TPU v7x, 32 devices: a whole 2x2x4 slice. The times are simulated.
32 devices in a mesh: img: 8 (over y, x, core), strip: 4 (over z).
Axes of the slice: x: 2, y: 2, z: 4, core: 2. Of those that a mesh axis runs over, the one named last changes fastest.
Arguments:
- pixels: bfloat16 [16, 48, 32, 3072], P('img', 'strip'), may hold values from -6 to 6
- cotangent: bfloat16 [16, 48, 32, 768], P('img', 'strip'), may hold values from -1.5 to 1.5
- resize: float32 [4, 32, 32], replicated, may hold values from -1 to 1
- patch_index: int32 [16], replicated, may hold values from 0 to 3
- slot_image: int32 [16], replicated, may hold values from 0 to 15, each once
- strip_rows: int32 [16, 4], replicated, may hold values from 1 to 12, 32 in all within a row
- patch_weight: bfloat16 [3072, 768], P(('img', 'strip')), may hold values from -0.109375 to 0.109375
- pos_grid: bfloat16 [49, 768], P(None, ('img', 'strip')), may hold values from -3 to 3
- patch_bias: bfloat16 [768], P(('img', 'strip')), may hold values from -1 to 1
- attention_norm_gain: bfloat16 [768], P(('img', 'strip')), may hold values from 0.5 to 1.5
- attn_shift: bfloat16 [768], P(('img', 'strip')), may hold values from -0.5 to 0.5
- query_weight: bfloat16 [768, 768], P(('img', 'strip')), may hold values from -0.21875 to 0.21875
- query_bias: bfloat16 [768], P(('img', 'strip')), may hold values from -1 to 1
- key_weight: bfloat16 [768, 768], P(('img', 'strip')), may hold values from -0.21875 to 0.21875
- value_weight: bfloat16 [768, 768], P(('img', 'strip')), may hold values from -0.21875 to 0.21875
- value_bias: bfloat16 [768], P(('img', 'strip')), may hold values from -0.25 to 0.25
- out_weight: bfloat16 [768, 768], P(('img', 'strip')), may hold values from -3 to 3
- out_bias: bfloat16 [768], P(('img', 'strip')), may hold values from -2.5 to 2.5
- mlp_gain: bfloat16 [768], P(('img', 'strip')), may hold values from 0.099609375 to 1.8984375
- mlp_shift: bfloat16 [768], P(('img', 'strip')), may hold values from -1.5 to 1.5
- up_weight: bfloat16 [768, 3072], P(('img', 'strip')), may hold values from -0.21875 to 0.21875
- up_bias: bfloat16 [3072], P(('img', 'strip')), may hold values from -1 to 1
- down_weight: bfloat16 [3072, 768], P(('img', 'strip')), may hold values from -0.109375 to 0.109375
- down_bias: bfloat16 [768], P(('img', 'strip')), may hold values from -2.5 to 2.5
Outputs:
- block_out: bfloat16 [16, 48, 32, 768], P('img', 'strip')
- pixel_grad: float32 [16, 48, 32, 3072], P('img', 'strip')
- grad_patch_weight: float32 [3072, 768], P(('img', 'strip'))
- grad_pos_grid: float32 [49, 768], P(None, ('img', 'strip'))
- grad_patch_bias: float32 [768], P(('img', 'strip'))
- grad_attn_gain: float32 [768], P(('img', 'strip'))
- grad_attn_shift: float32 [768], P(('img', 'strip'))
- grad_query_weight: float32 [768, 768], P(('img', 'strip'))
- grad_query_bias: float32 [768], P(('img', 'strip'))
- grad_key_weight: float32 [768, 768], P(('img', 'strip'))
- grad_value_weight: float32 [768, 768], P(('img', 'strip'))
- grad_value_bias: float32 [768], P(('img', 'strip'))
- output_weight_gradient: float32 [768, 768], P(('img', 'strip'))
- grad_out_bias: float32 [768], P(('img', 'strip'))
- grad_mlp_gain: float32 [768], P(('img', 'strip'))
- grad_mlp_shift: float32 [768], P(('img', 'strip'))
- grad_up_weight: float32 [768, 3072], P(('img', 'strip'))
- grad_up_bias: float32 [3072], P(('img', 'strip'))
- grad_down_weight: float32 [3072, 768], P(('img', 'strip'))
- grad_down_bias: float32 [768], P(('img', 'strip'))
Inputs may be any that keep to these rules, and one draw needn't show every extreme that they name: `patch_index`: the patch size of an image is (its index + 1) * 8 pixels. `slot_image`: every image is held by exactly one slot. `strip_rows`: each slot's entries sum to 32; in every draw some entry equals 12.
All inputs are finite; a program needn't handle non-finite values.
Results may differ from a plain program's by a relative error of at most 0.015.
Values may be sent and summed in bfloat16 or wider, within the bound.
No kernel may reach another device: no remote copies, remote signals or barrier semaphores. Data moves between devices by JAX's collectives and lax.ppermute only.
A program may use at most 256 MiB of HBM per device.

v0:
```python
import jax
import jax.numpy as jnp
from jax import lax
from jax.sharding import PartitionSpec as P

HEADS = 12
BASE = 7


HIGH_ACCURACY = lax.Precision.HIGHEST


def bilinear(out_count, in_count):
    source = (jnp.arange(out_count).astype(jnp.float32) + 0.5) * (in_count / out_count) - 0.5
    source = jnp.clip(source, 0.0, in_count - 1.0)
    target = jnp.arange(in_count).astype(jnp.float32)
    return jnp.maximum(1.0 - jnp.abs(source[:, None] - target[None, :]), 0.0)


def layer_norm(values, gain, shift):
    centred = values - jnp.mean(values, axis=-1, keepdims=True)
    token_spread = jnp.mean(centred * centred, axis=-1, keepdims=True)
    return centred * lax.rsqrt(token_spread + 1e-06) * gain + shift


def gelu_exact(values):
    return jax.nn.gelu(values, approximate=False)


def matmul(left, right):
    return jnp.dot(left, right, preferred_element_type=jnp.float32)


def left_trans(left, right):
    return lax.dot_general(
        left, right, (((0,), (0,)), ((), ())), preferred_element_type=jnp.float32
    )


def right_trans(left, right):
    return lax.dot_general(
        left, right, (((1,), (1,)), ((), ())), preferred_element_type=jnp.float32
    )


def split_heads(values, heads):
    group, length, width = values.shape
    return values.reshape(group, length, heads, width // heads).transpose(2, 0, 1, 3)


def join_heads(values):
    heads, group, length, size = values.shape
    return values.transpose(1, 2, 0, 3).reshape(group, length, heads * size)


def body(
    pixels,
    cotangent,
    resize,
    patch_index,
    slot_image,
    strip_rows,
    patch_weight,
    pos_grid,
    patch_bias,
    attention_norm_gain,
    attn_shift,
    query_weight,
    query_bias,
    key_weight,
    value_weight,
    value_bias,
    out_weight,
    out_bias,
    mlp_gain,
    mlp_shift,
    up_weight,
    up_bias,
    down_weight,
    down_bias,
):
    group, capacity, grid, pixel_len = pixels.shape
    width = cotangent.shape[3]
    local_rows = capacity * grid
    tokens = group * local_rows
    strips = lax.axis_size("strip")
    here = lax.axis_index("strip")
    first_slot = lax.axis_index("img") * group
    f32 = jnp.float32
    bf16 = jnp.bfloat16
    full = (
        lax.all_gather(patch_weight, ("img", "strip"), axis=0, tiled=True),
        lax.all_gather(pos_grid, ("img", "strip"), axis=1, tiled=True),
        lax.all_gather(patch_bias, ("img", "strip"), axis=0, tiled=True),
        lax.all_gather(attention_norm_gain, ("img", "strip"), axis=0, tiled=True),
        lax.all_gather(attn_shift, ("img", "strip"), axis=0, tiled=True),
        lax.all_gather(query_weight, ("img", "strip"), axis=0, tiled=True),
        lax.all_gather(query_bias, ("img", "strip"), axis=0, tiled=True),
        lax.all_gather(key_weight, ("img", "strip"), axis=0, tiled=True),
        lax.all_gather(value_weight, ("img", "strip"), axis=0, tiled=True),
        lax.all_gather(value_bias, ("img", "strip"), axis=0, tiled=True),
        lax.all_gather(out_weight, ("img", "strip"), axis=0, tiled=True),
        lax.all_gather(out_bias, ("img", "strip"), axis=0, tiled=True),
        lax.all_gather(mlp_gain, ("img", "strip"), axis=0, tiled=True),
        lax.all_gather(mlp_shift, ("img", "strip"), axis=0, tiled=True),
        lax.all_gather(up_weight, ("img", "strip"), axis=0, tiled=True),
        lax.all_gather(up_bias, ("img", "strip"), axis=0, tiled=True),
        lax.all_gather(down_weight, ("img", "strip"), axis=0, tiled=True),
        lax.all_gather(down_bias, ("img", "strip"), axis=0, tiled=True),
    )
    (
        w_patch,
        grid_pos,
        b_patch,
        g_one,
        c_one,
        w_query,
        b_query,
        w_key,
        w_value,
        b_value,
        w_out,
        b_out,
        g_two,
        c_two,
        w_up,
        b_up,
        w_down,
        b_down,
    ) = full
    size_count = resize.shape[0]
    side = resize.shape[1]
    step_px = side // size_count
    slot_ids = lax.dynamic_slice_in_dim(slot_image, first_slot, group)
    picked = slot_ids[:, None] == jnp.arange(patch_index.shape[0], dtype=jnp.int32)[None, :]
    size_index = jnp.sum(jnp.where(picked, patch_index[None, :], 0), axis=1)
    choose = (size_index[:, None] == jnp.arange(size_count, dtype=jnp.int32)[None, :]).astype(f32)
    tables = jnp.einsum("gs,sij->gij", choose, resize, precision=HIGH_ACCURACY)
    limit = step_px * (size_index + 1)
    tables = (
        tables
        * (jnp.arange(side, dtype=jnp.int32)[None, :] < limit[:, None]).astype(f32)[:, :, None]
    )
    mixers = (
        (tables[:, :, None, :, None] * tables[:, None, :, None, :])
        .reshape(group, side * side, side * side)
        .astype(bf16)
    )
    counts = lax.dynamic_slice_in_dim(strip_rows, first_slot, group, 0)
    strip_iota = jnp.arange(strips, dtype=jnp.int32)[None, :]
    rows_here = jnp.sum(jnp.where(strip_iota == here, counts, 0), axis=1)
    start_here = jnp.sum(jnp.where(strip_iota < here, counts, 0), axis=1)
    row_iota = jnp.arange(capacity, dtype=jnp.int32)
    live = row_iota[None, :] < rows_here[:, None]
    token_live = jnp.broadcast_to(live[:, :, None], (group, capacity, grid)).reshape(tokens, 1)
    key_live = jnp.broadcast_to(
        (row_iota[None, None, :] < counts[:, :, None])[..., None], (group, strips, capacity, grid)
    ).reshape(group, 1, strips * local_rows)
    token_spread = bilinear(grid, BASE)
    global_row = start_here[:, None] + row_iota[None, :]
    selected_rows = (
        global_row[:, :, None] == jnp.arange(grid, dtype=jnp.int32)[None, None, :]
    ).astype(f32)
    local_token_spread = jnp.einsum(
        "ymd,dn->ymn", selected_rows, token_spread, precision=HIGH_ACCURACY
    )
    pix_rows = pixels.reshape(group, local_rows, 3, side * side)
    mixed = jnp.einsum("gtcj,gjk->gtck", pix_rows, mixers, preferred_element_type=f32)
    base_pixels = mixed.reshape(tokens, pixel_len).astype(bf16)
    place = jnp.einsum(
        "gra,hb,abd->grhd",
        local_token_spread,
        token_spread,
        grid_pos.astype(f32).reshape(BASE, BASE, width),
        precision=HIGH_ACCURACY,
    ).reshape(tokens, width)
    embed = matmul(base_pixels, w_patch) + b_patch.astype(f32) + place
    normed_one, norm_one_back = jax.vjp(layer_norm, embed, g_one.astype(f32), c_one.astype(f32))
    attn_in = normed_one.astype(bf16)
    query = ((matmul(attn_in, w_query) + b_query.astype(f32)) * 0.125).astype(bf16)
    key_rows = matmul(attn_in, w_key).astype(bf16).reshape(group, local_rows, width)
    value_rows = (
        (matmul(attn_in, w_value) + b_value.astype(f32))
        .astype(bf16)
        .reshape(group, local_rows, width)
    )
    keys_all, values_all = (
        lax.all_gather(key_rows, "strip", axis=1, tiled=True),
        lax.all_gather(value_rows, "strip", axis=1, tiled=True),
    )
    heads = HEADS
    query_rows = query.reshape(group, local_rows, width)
    q_heads = split_heads(query_rows, heads)

    def head_forward(parts):
        q_head, k_head, v_head = parts
        scores = jnp.einsum("gqd,gkd->gqk", q_head, k_head, preferred_element_type=f32)
        scores = jnp.where(key_live, scores, -1e30)
        peak = jnp.max(scores, axis=-1, keepdims=True)
        expd = jnp.exp(scores - peak)
        denom = jnp.sum(expd, axis=-1, keepdims=True)
        probs = (expd / denom).astype(bf16)
        result = jnp.einsum("gqk,gkd->gqd", probs, v_head, preferred_element_type=f32)
        return (result, peak + jnp.log(denom))

    head_outs, log_sums = lax.map(
        head_forward, (q_heads, split_heads(keys_all, heads), split_heads(values_all, heads))
    )
    attended = join_heads(head_outs).reshape(tokens, width).astype(bf16)
    resid = embed + matmul(attended, w_out) + b_out.astype(f32)
    normed_two, norm_two_back = jax.vjp(layer_norm, resid, g_two.astype(f32), c_two.astype(f32))
    mlp_in = normed_two.astype(bf16)
    upper = matmul(mlp_in, w_up) + b_up.astype(f32)
    activ, gelu_back = jax.vjp(gelu_exact, upper)
    hidden_features = activ.astype(bf16)
    final = resid + matmul(hidden_features, w_down) + b_down.astype(f32)
    block_out = jnp.where(token_live, final, 0.0).astype(bf16).reshape(cotangent.shape)
    bw_patch = full[0]
    bw_query = full[5]
    bw_key = full[7]
    bw_value = full[8]
    bw_out = full[10]
    bw_up = full[14]
    bw_down = full[16]
    g_out = jnp.where(token_live, cotangent.reshape(tokens, width).astype(f32), 0.0)
    grad_down_bias = jnp.sum(g_out, axis=0)
    g_out_low = g_out.astype(bf16)
    grad_down_weight = left_trans(hidden_features, g_out_low)
    (g_upper,) = gelu_back(right_trans(g_out_low, bw_down))
    grad_up_bias = jnp.sum(g_upper, axis=0)
    g_upper_low = g_upper.astype(bf16)
    grad_up_weight = left_trans(mlp_in, g_upper_low)
    g_resid_norm, grad_mlp_gain, grad_mlp_shift = norm_two_back(right_trans(g_upper_low, bw_up))
    g_resid = g_out + g_resid_norm
    grad_out_bias = jnp.sum(g_resid, axis=0)
    g_resid_low = g_resid.astype(bf16)
    output_weight_gradient = left_trans(attended, g_resid_low)
    g_att = right_trans(g_resid_low, bw_out).astype(bf16).reshape(group, local_rows, width)
    keys_back, values_back = (keys_all, values_all)

    def head_backward(parts):
        q_head, k_head, v_head, d_head, lse_head = parts
        scores = jnp.einsum("gqd,gkd->gqk", q_head, k_head, preferred_element_type=f32)
        scores = jnp.where(key_live, scores, -1e30)
        probs = jnp.exp(scores - lse_head)
        g_probs = jnp.einsum("gqd,gkd->gqk", d_head, v_head, preferred_element_type=f32)
        inner = jnp.sum(probs * g_probs, axis=-1, keepdims=True)
        g_scores = (probs * (g_probs - inner)).astype(bf16)
        g_query = jnp.einsum("gqk,gkd->gqd", g_scores, k_head, preferred_element_type=f32)
        g_key = jnp.einsum("gqk,gqd->gkd", g_scores, q_head, preferred_element_type=f32)
        g_value = jnp.einsum("gqk,gqd->gkd", probs.astype(bf16), d_head, preferred_element_type=f32)
        return (g_query, g_key, g_value, inner)

    g_q_heads, g_k_heads, g_v_heads, inners = lax.map(
        head_backward,
        (
            q_heads,
            split_heads(keys_back, heads),
            split_heads(values_back, heads),
            split_heads(g_att, heads),
            log_sums,
        ),
    )
    g_key_sum, g_value_sum = (
        lax.psum_scatter(
            join_heads(g_k_heads).astype(jnp.bfloat16), "strip", scatter_dimension=1, tiled=True
        ).astype(jnp.float32),
        lax.psum_scatter(
            join_heads(g_v_heads).astype(jnp.bfloat16), "strip", scatter_dimension=1, tiled=True
        ).astype(jnp.float32),
    )
    g_key_low = g_key_sum.reshape(tokens, width).astype(bf16)
    g_value_low = g_value_sum.reshape(tokens, width).astype(bf16)
    g_qin = join_heads(g_q_heads).reshape(tokens, width).astype(bf16).astype(f32) * 0.125
    grad_query_bias = jnp.sum(g_qin, axis=0)
    g_qin_low = g_qin.astype(bf16)
    grad_query_weight = left_trans(attn_in, g_qin_low)
    grad_key_weight = left_trans(attn_in, g_key_low)
    grad_value_weight = left_trans(attn_in, g_value_low)
    grad_value_bias = jnp.sum(g_value_low.astype(f32), axis=0)
    g_norm_in = (
        right_trans(g_qin_low, bw_query)
        + right_trans(g_key_low, bw_key)
        + right_trans(g_value_low, bw_value)
    )
    g_embed_norm, grad_attn_gain, grad_attn_shift = norm_one_back(g_norm_in)
    g_embed = g_resid + g_embed_norm
    grad_patch_bias = jnp.sum(g_embed, axis=0)
    grad_pos_grid = jnp.einsum(
        "gra,hb,grhd->abd",
        local_token_spread,
        token_spread,
        g_embed.reshape(group, capacity, grid, width),
        precision=HIGH_ACCURACY,
    ).reshape(BASE * BASE, width)
    g_embed_low = g_embed.astype(bf16)
    grad_patch_weight = left_trans(base_pixels, g_embed_low)
    g_base = (
        right_trans(g_embed_low, bw_patch).astype(bf16).reshape(group, local_rows, 3, side * side)
    )
    pixel_grad = jnp.einsum("gtck,gjk->gtcj", g_base, mixers, preferred_element_type=f32).reshape(
        pixels.shape
    )
    summed = (
        lax.psum_scatter(grad_patch_weight, ("img", "strip"), scatter_dimension=0, tiled=True),
        lax.psum_scatter(grad_pos_grid, ("img", "strip"), scatter_dimension=1, tiled=True),
        lax.psum_scatter(grad_patch_bias, ("img", "strip"), scatter_dimension=0, tiled=True),
        lax.psum_scatter(grad_attn_gain, ("img", "strip"), scatter_dimension=0, tiled=True),
        lax.psum_scatter(grad_attn_shift, ("img", "strip"), scatter_dimension=0, tiled=True),
        lax.psum_scatter(grad_query_weight, ("img", "strip"), scatter_dimension=0, tiled=True),
        lax.psum_scatter(grad_query_bias, ("img", "strip"), scatter_dimension=0, tiled=True),
        lax.psum_scatter(grad_key_weight, ("img", "strip"), scatter_dimension=0, tiled=True),
        lax.psum_scatter(grad_value_weight, ("img", "strip"), scatter_dimension=0, tiled=True),
        lax.psum_scatter(grad_value_bias, ("img", "strip"), scatter_dimension=0, tiled=True),
        lax.psum_scatter(output_weight_gradient, ("img", "strip"), scatter_dimension=0, tiled=True),
        lax.psum_scatter(grad_out_bias, ("img", "strip"), scatter_dimension=0, tiled=True),
        lax.psum_scatter(grad_mlp_gain, ("img", "strip"), scatter_dimension=0, tiled=True),
        lax.psum_scatter(grad_mlp_shift, ("img", "strip"), scatter_dimension=0, tiled=True),
        lax.psum_scatter(grad_up_weight, ("img", "strip"), scatter_dimension=0, tiled=True),
        lax.psum_scatter(grad_up_bias, ("img", "strip"), scatter_dimension=0, tiled=True),
        lax.psum_scatter(grad_down_weight, ("img", "strip"), scatter_dimension=0, tiled=True),
        lax.psum_scatter(grad_down_bias, ("img", "strip"), scatter_dimension=0, tiled=True),
    )
    return (
        block_out,
        pixel_grad,
        summed[0],
        summed[1],
        summed[2],
        summed[3],
        summed[4],
        summed[5],
        summed[6],
        summed[7],
        summed[8],
        summed[9],
        summed[10],
        summed[11],
        summed[12],
        summed[13],
        summed[14],
        summed[15],
        summed[16],
        summed[17],
    )


def solution(mesh):
    return jax.shard_map(
        body,
        mesh=mesh,
        in_specs=(
            P("img", "strip", None, None),
            P("img", "strip", None, None),
            P(),
            P(),
            P(),
            P(),
            P(("img", "strip"), None),
            P(None, ("img", "strip")),
            P(("img", "strip")),
            P(("img", "strip")),
            P(("img", "strip")),
            P(("img", "strip"), None),
            P(("img", "strip")),
            P(("img", "strip"), None),
            P(("img", "strip"), None),
            P(("img", "strip")),
            P(("img", "strip"), None),
            P(("img", "strip")),
            P(("img", "strip")),
            P(("img", "strip")),
            P(("img", "strip"), None),
            P(("img", "strip")),
            P(("img", "strip"), None),
            P(("img", "strip")),
        ),
        out_specs=(
            P("img", "strip", None, None),
            P("img", "strip", None, None),
            P(("img", "strip"), None),
            P(None, ("img", "strip")),
            P(("img", "strip")),
            P(("img", "strip")),
            P(("img", "strip")),
            P(("img", "strip"), None),
            P(("img", "strip")),
            P(("img", "strip"), None),
            P(("img", "strip"), None),
            P(("img", "strip")),
            P(("img", "strip"), None),
            P(("img", "strip")),
            P(("img", "strip")),
            P(("img", "strip")),
            P(("img", "strip"), None),
            P(("img", "strip")),
            P(("img", "strip"), None),
            P(("img", "strip")),
        ),
        check_vma=False,
    )
```

profile of v0, /device:TPU:0, one launch (start us, length us, event | category | flops | bytes accessed | tf_op | source)
XLA Modules:
  0.0 1990.3 jit_solution(15464815552199330778)
XLA Ops:
  20.9 43.0 %all-reduce.22 = (bf16[768]{0:T(1024)(128)(2,1)S(1)}, bf16[768]{0:T(1024)(128)(2,1)S(1)}, bf16[768]{0:T(1024)(128)(2,1)S(1)}, bf16[768]{0:T(1024)(128)(2,1)S(1)}...) all-reduce(bf16[768]{0:T(1024)(128)(2,1)S(1)} %dynamic-update-slice, ...), channel_id=1, replica_groups=mesh['img'=8,'strip'=4] {'img','strip'}, use_global_device_ids=true, to_apply=%add | all-reduce | flops 9984 | bytes 39936
  64.3 68.2 %all_gather.62 = bf16[49,768]{0,1:T(8,128)(2,1)S(1)} all-gather(bf16[49,24]{0,1:T(8,128)(2,1)} %param.35), channel_id=1, replica_groups=mesh['img'=8,'strip'=4] {'img','strip'}, dimensions={1}, use_global_device_ids=true | all-gather | bytes 77616 | tf_op jit(solution)/shard_map/all_gather | solution.py:93
  156.9 23.3 %convert_element_type.196 = bf16[2,1024,1024]{2,1,0:T(8,128)(2,1)} reshape(bf16[2,32,32,32,32]{4,3,2,1,0:T(8,128)(2,1)} %multiply_convert_fusion.1) | data formatting | bytes 8388608 | tf_op jit(solution)/shard_map/convert_element_type | solution.py:147
  180.3 14.1 convert_bitcast_fusion
  258.1 77.3 %all-gather.20.cloned.1.call-done = bf16[2,1536,768]{1,2,0:T(8,128)(2,1)} async-done(((bf16[2,384,768]{1,2,0:T(8,128)(2,1)}), bf16[2,1536,768]{1,2,0:T(8,128)(2,1)}) %all-gather.20.cloned.1.call-update) | async-done | bytes 4718608 | tf_op jit(solution)/shard_map/all_gather | solution.py:189
  340.3 84.4 %all-gather.16.cloned.1.call-done = bf16[2,1536,768]{1,2,0:T(8,128)(2,1)} async-done(((bf16[2,384,768]{1,2,0:T(8,128)(2,1)}), bf16[2,1536,768]{1,2,0:T(8,128)(2,1)}) %all-gather.16.cloned.1.call-update) | async-done | bytes 4718608 | tf_op jit(solution)/shard_map/all_gather | solution.py:188
  430.9 78.2 %while.28 = (s32[]{:T(128)}, bf16[12,2,384,64]{2,3,1,0:T(8,128)(2,1)}, f32[12,2,384,1]{2,1,3,0:T(2,128)}, bf16[12,2,384,64]{2,3,1,0:T(8,128)(2,1)}, bf16[12,2,15...) while((s32[]{:T(128)}, ...), condition=%wide.region_8.9_spmd.clone, body=%wide.region_5.8_spmd.clone.sunk | while | flops 312605952 | bytes 15282369 | solution.py:206
  517.7 27.8 %all-gather.24.cloned.1.call-done = bf16[768,3072]{1,0:T(8,128)(2,1)} async-done(((bf16[24,3072]{1,0:T(8,128)(2,1)}), bf16[768,3072]{1,0:T(8,128)(2,1)}) %all-gather.24.cloned.1.call-update) | async-done | bytes 4718608 | tf_op jit(solution)/shard_map/all_gather | solution.py:106
  556.3 54.5 %all-gather.26.cloned.1.call-done = bf16[3072,768]{1,0:T(8,128)(2,1)} async-done(((bf16[96,768]{1,0:T(8,128)(2,1)}), bf16[3072,768]{1,0:T(8,128)(2,1)}) %all-gather.26.cloned.1.call-update) | async-done | bytes 4718608 | tf_op jit(solution)/shard_map/all_gather | solution.py:108
  610.7 31.1 %fusion.108 = (f32[3072]{0:T(1024)}, bf16[768,3072]{1,0:T(8,128)(2,1)S(1)}, f32[768,3072]{1,0:T(8,128)}) fusion(f32[768,3072]{1,0:T(8,128)} %fusion.107, f32[3072]{0:T(1024)S(1)} %convert_element_type.218, bf16[768,768]{1,0:T(8,128)(2,1)} %fusion.59, bf16[3072,768]{1,0:T(8,128)(2,1)} %all-gather.26.cloned.1.call-done), kind=kOutput, calls=%fused_computation.181 | convolution fusion | flops 3798463488 | bytes 29515776 | tf_op jit(solution)/shard_map/dot_general | solution.py:41
  659.8 150.4 %while.29 = (s32[]{:T(128)}, bf16[12,2,384,64]{2,3,1,0:T(8,128)(2,1)}, bf16[12,2,1536,64]{2,3,0,1:T(8,128)(2,1)}, bf16[12,2,1536,64]{2,3,0,1:T(8,128)(2,1)}, bf1...) while((s32[]{:T(128)}, ...), condition=%wide.region_15.16_spmd.clone, body=%wide.region_13.15_spmd.clone.sunk | while | flops 764411136 | bytes 38959332 | solution.py:254
  853.0 59.4 %reduce-scatter.31.cloned.1.call-done = bf16[384,1536]{1,0:T(8,128)(2,1)} async-done(((bf16[1536,1536]{1,0:T(8,128)(2,1)}), bf16[384,1536]{1,0:T(8,128)(2,1)}) %reduce-scatter.31.cloned.1.call-update) | async-done | bytes 1179664
  918.6 81.9 %reduce-scatter.29.cloned.1.call-done = bf16[384,1536]{1,0:T(8,128)(2,1)} async-done(((bf16[1536,1536]{1,0:T(8,128)(2,1)}), bf16[384,1536]{1,0:T(8,128)(2,1)}) %reduce-scatter.29.cloned.1.call-update) | async-done | bytes 1179664
  1076.9 23.3 %reshape.353 = bf16[2,1024,1024,1]{2,1,0,3:T(8,128)(2,1)} reshape(bf16[2,32,32,32,32]{4,3,2,1,0:T(8,128)(2,1)} %multiply_convert_fusion.1) | data formatting | bytes 8388608 | tf_op jit(solution)/shard_map/convert_element_type | solution.py:147
  1117.0 41.9 %all-reduce.21 = (f32[768]{0:T(1024)S(1)}, f32[768]{0:T(1024)S(1)}, f32[768]{0:T(1024)S(1)}, f32[768]{0:T(1024)S(1)}, f32[768]{0:T(1024)S(1)}, /*index=5*/f32[76...) all-reduce(f32[768]{0:T(1024)S(1)} %get-tuple-element.372, ...), channel_id=6, replica_groups=mesh['img'=8,'strip'=4] {'img','strip'}, use_global_device_ids=true, to_apply=%region_23.24.clone | all-reduce | flops 9984 | bytes 79872
  1196.4 16.9 copy.176
  1213.3 16.1 reshape.315
  1231.5 15.2 reduce-scatter.23.cloned.1.call-done
  1246.7 104.6 %reduce-scatter.17.cloned.1.call-done = f32[24,768]{1,0:T(8,128)} async-done(((f32[768,768]{1,0:T(8,128)}), f32[24,768]{1,0:T(8,128)}) %reduce-scatter.17.cloned.1.call-update) | async-done | bytes 73744 | tf_op jit(solution)/shard_map/reduce_scatter | solution.py:310
  1351.4 140.9 %reduce-scatter.25.cloned.1.call-done = f32[24,3072]{1,0:T(8,128)} async-done(((f32[768,3072]{1,0:T(8,128)}), f32[24,3072]{1,0:T(8,128)}) %reduce-scatter.25.cloned.1.call-update) | async-done | bytes 294928 | tf_op jit(solution)/shard_map/reduce_scatter | solution.py:319
  1492.2 141.9 %reduce-scatter.27.cloned.1.call-done = f32[96,768]{1,0:T(8,128)} async-done(((f32[3072,768]{1,0:T(8,128)}), f32[96,768]{1,0:T(8,128)}) %reduce-scatter.27.cloned.1.call-update) | async-done | bytes 294928 | tf_op jit(solution)/shard_map/reduce_scatter | solution.py:321
  1634.1 103.9 %reduce-scatter.21.cloned.1.call-done = f32[24,768]{1,0:T(8,128)} async-done(((f32[768,768]{1,0:T(8,128)}), f32[24,768]{1,0:T(8,128)}) %reduce-scatter.21.cloned.1.call-update) | async-done | bytes 73744 | tf_op jit(solution)/shard_map/reduce_scatter | solution.py:313
  1738.0 104.7 %reduce-scatter.19.cloned.1.call-done = f32[24,768]{1,0:T(8,128)} async-done(((f32[768,768]{1,0:T(8,128)}), f32[24,768]{1,0:T(8,128)}) %reduce-scatter.19.cloned.1.call-update) | async-done | bytes 73744 | tf_op jit(solution)/shard_map/reduce_scatter | solution.py:312
  1842.6 140.9 %reduce-scatter.15.cloned.1.call-done = f32[96,768]{1,0:T(8,128)} async-done(((f32[3072,768]{1,0:T(8,128)}), f32[96,768]{1,0:T(8,128)}) %reduce-scatter.15.cloned.1.call-update) | async-done | bytes 294928 | tf_op jit(solution)/shard_map/reduce_scatter | solution.py:305
  (473 shorter events, 559.3 us)
Async XLA Ops:
  7.2 201.9 %all-gather.10.cloned.1.call-start = ((), (), s32[]{:S(2)}) async-start(), calls=%async_computation.9 | async-start | bytes 4866048 | tf_op jit(solution)/shard_map/all_gather | solution.py:92
  7.9 211.6 %all-gather.18.cloned.1.call-start = ((), (), s32[]{:S(2)}) async-start(), calls=%async_computation.13 | async-start | bytes 1216512 | tf_op jit(solution)/shard_map/all_gather | solution.py:100
  8.7 217.2 %all-gather.14.cloned.1.call-start = ((), (), s32[]{:S(2)}) async-start(), calls=%async_computation.11 | async-start | bytes 1216512 | tf_op jit(solution)/shard_map/all_gather | solution.py:99
  9.4 236.2 %all-gather.12.cloned.1.call-start = ((), (), s32[]{:S(2)}) async-start(), calls=%async_computation.10 | async-start | bytes 1216512 | tf_op jit(solution)/shard_map/all_gather | solution.py:97
  10.0 325.4 %all-gather.20.cloned.1.call-start = ((), (), s32[]{:S(2)}) async-start(), calls=%async_computation.14 | async-start | bytes 5898240 | tf_op jit(solution)/shard_map/all_gather | solution.py:189
  10.1 127.0 %copy-start.40 = (f32[32]{0:T(128)}, f32[32]{0:T(128)S(1)}, u32[]{:S(2)}) copy-start(f32[32]{0:T(128)S(1)} %add_clamp_fusion) | copy-start | bytes 388
  64.0 154.1 %copy-start.23 = (f32[768]{0:T(1024)}, f32[768]{0:T(1024)S(1)}, u32[]{:S(2)}) copy-start(f32[768]{0:T(1024)S(1)} %convert_element_type.203) | copy-start | bytes 9220
  217.6 295.3 %copy-start.2 = (f32[768,768]{1,0:T(8,128)}, f32[768,768]{1,0:T(8,128)S(1)}, u32[]{:S(2)}) copy-start(f32[768,768]{1,0:T(8,128)S(1)} %get-tuple-element.386) | copy-start | bytes 7077892
  225.7 199.0 %all-gather.16.cloned.1.call-start = ((), (), s32[]{:S(2)}) async-start(), calls=%async_computation.12 | async-start | bytes 5898240 | tf_op jit(solution)/shard_map/all_gather | solution.py:188
  232.1 280.8 %all-gather.22.cloned.1.call-start = ((), (), s32[]{:S(2)}) async-start(), calls=%async_computation.15 | async-start | bytes 1216512 | tf_op jit(solution)/shard_map/all_gather | solution.py:102
  232.8 312.7 %all-gather.24.cloned.1.call-start = ((), (), s32[]{:S(2)}) async-start(), calls=%async_computation.16 | async-start | bytes 4866048 | tf_op jit(solution)/shard_map/all_gather | solution.py:106
  233.6 377.2 %all-gather.26.cloned.1.call-start = ((), (), s32[]{:S(2)}) async-start(), calls=%async_computation.17 | async-start | bytes 4866048 | tf_op jit(solution)/shard_map/all_gather | solution.py:108
  234.3 678.1 %reduce-scatter.31.cloned.1.call-start = ((), (), s32[]{:S(2)}) async-start(), calls=%async_computation.26 | async-start | bytes 5898240
  234.8 310.7 %copy-start.17 = (f32[768]{0:T(1024)}, f32[768]{0:T(1024)S(1)}, u32[]{:S(2)}) copy-start(f32[768]{0:T(1024)S(1)} %convert_element_type.216) | copy-start | bytes 9220
  828.2 172.3 %reduce-scatter.29.cloned.1.call-start = ((), (), s32[]{:S(2)}) async-start(), calls=%async_computation.25 | async-start | bytes 5898240
  846.2 383.8 %all-reduce.25.cloned.1.call-start = ((), (), s32[]{:S(2)}) async-start(), calls=%async_computation.27 | async-start | bytes 344064
  1017.2 229.5 %reduce-scatter.23.cloned.1.call-start = ((), (), s32[]{:S(2)}) async-start(), calls=%async_computation.22 | async-start | bytes 2433024 | tf_op jit(solution)/shard_map/reduce_scatter | solution.py:315
  1021.9 329.5 %reduce-scatter.17.cloned.1.call-start = ((), (), s32[]{:S(2)}) async-start(), calls=%async_computation.19 | async-start | bytes 2433024 | tf_op jit(solution)/shard_map/reduce_scatter | solution.py:310
  1026.1 466.1 %reduce-scatter.25.cloned.1.call-start = ((), (), s32[]{:S(2)}) async-start(), calls=%async_computation.23 | async-start | bytes 9732096 | tf_op jit(solution)/shard_map/reduce_scatter | solution.py:319
  1035.7 598.4 %reduce-scatter.27.cloned.1.call-start = ((), (), s32[]{:S(2)}) async-start(), calls=%async_computation.24 | async-start | bytes 9732096 | tf_op jit(solution)/shard_map/reduce_scatter | solution.py:321
  1057.3 680.6 %reduce-scatter.21.cloned.1.call-start = ((), (), s32[]{:S(2)}) async-start(), calls=%async_computation.21 | async-start | bytes 2433024 | tf_op jit(solution)/shard_map/reduce_scatter | solution.py:313
  1061.6 781.1 %reduce-scatter.19.cloned.1.call-start = ((), (), s32[]{:S(2)}) async-start(), calls=%async_computation.20 | async-start | bytes 2433024 | tf_op jit(solution)/shard_map/reduce_scatter | solution.py:312
  1065.8 917.7 %reduce-scatter.15.cloned.1.call-start = ((), (), s32[]{:S(2)}) async-start(), calls=%async_computation.18 | async-start | bytes 9732096 | tf_op jit(solution)/shard_map/reduce_scatter | solution.py:305
  1213.3 770.2 %copy-start.1 = (f32[4,32,32]{2,1,0:T(8,128)S(1)}, f32[4,32,32]{2,1,0:T(8,128)}, u32[]{:S(2)}) copy-start(f32[4,32,32]{2,1,0:T(8,128)} %param.30) | copy-start | bytes 49156
  (43 other events, 545.8 us)
Sparse Core Ops, SparseCore 0:
  10.8 67.8 all-gather.9
  81.5 52.4 all-gather.17
  136.8 52.9 all-gather.13
  192.5 53.0 all-gather.11
  247.0 88.2 all-gather.19
  336.8 87.8 all-gather.15
  427.5 52.6 all-gather.21
  483.0 62.4 all-gather.23
  548.3 62.3 all-gather.25
  828.3 84.0 reduce-scatter.30
  914.7 85.7 reduce-scatter.28
  1017.3 122.4 all-reduce.24
  1145.7 101.0 reduce-scatter.22
  1253.3 98.0 reduce-scatter.16
  1357.7 134.5 reduce-scatter.24
  1499.6 134.4 reduce-scatter.26
  1639.8 98.1 reduce-scatter.20
  1744.5 98.0 reduce-scatter.18
  1849.1 134.3 reduce-scatter.14
where the time goes:
time: 2000 us; the launch traced here: 1990 us
  waiting for transfers between devices  1150 us (58%)
  matrix products  351 us (18%)
  local copies, waits for them, and re-layouts  262 us (13%)
  blocking collectives  153 us (8%)
  other arithmetic  56.1 us (3%)
    unnamed x22, waiting for transfers between devices  146 us
    reduce_scatter x1, waiting for transfers between devices, body(): lax.psum_scatter(grad_down_weight, ('img', 'strip'), scatter_dimension=0,...  142 us
    reduce_scatter x1, waiting for transfers between devices, body(): lax.psum_scatter(grad_patch_weight, ('img', 'strip'), scatter_dimension=0...  141 us
    reduce_scatter x1, waiting for transfers between devices, body(): lax.psum_scatter(grad_up_weight, ('img', 'strip'), scatter_dimension=0, t...  141 us
    reduce_scatter x1, waiting for transfers between devices, body(): lax.psum_scatter(grad_key_weight, ('img', 'strip'), scatter_dimension=0,...  105 us
    reduce_scatter x1, waiting for transfers between devices, body(): lax.psum_scatter(grad_query_weight, ('img', 'strip'), scatter_dimension=0...  105 us
    reduce_scatter x1, waiting for transfers between devices, body(): lax.psum_scatter(grad_value_weight, ('img', 'strip'), scatter_dimension=0...  104 us
    unnamed x141, local copies, waits for them, and re-layouts  92.9 us
  transfers between devices with their start and end apart: 19, of which 14 were waited for; matrix products, arithmetic and copies ran while one was open for 22% of the time, Pallas kernels for 0%

commit v1 on v0

v1 whole, which is shorter than its diff:
```python
import jax
import jax.numpy as jnp
import numpy as np
from jax import lax
from jax.sharding import PartitionSpec as P

HEADS = 12
BASE = 7
HIGH_ACCURACY = lax.Precision.HIGHEST
AXES = ("img", "strip")


def bilinear(out_count, in_count):
    source = (np.arange(out_count, dtype=np.float32) + 0.5) * (in_count / out_count) - 0.5
    source = np.clip(source, 0.0, in_count - 1.0)
    target = np.arange(in_count, dtype=np.float32)
    return np.maximum(1.0 - np.abs(source[:, None] - target[None, :]), 0.0).astype(np.float32)


def layer_norm(values, gain, shift):
    centred = values - jnp.mean(values, axis=-1, keepdims=True)
    token_spread = jnp.mean(centred * centred, axis=-1, keepdims=True)
    return centred * lax.rsqrt(token_spread + 1e-06) * gain + shift


def gelu_exact(values):
    return jax.nn.gelu(values, approximate=False)


def matmul(left, right):
    return jnp.dot(left, right, preferred_element_type=jnp.float32)


def left_trans(left, right):
    return lax.dot_general(
        left, right, (((0,), (0,)), ((), ())), preferred_element_type=jnp.float32
    )


def right_trans(left, right):
    return lax.dot_general(
        left, right, (((1,), (1,)), ((), ())), preferred_element_type=jnp.float32
    )


class Place:
    def __init__(self, group):
        self.group = group
        self.images = lax.axis_size("img")
        self.strips = lax.axis_size("strip")
        assert 2 * group == self.strips
        self.img = lax.axis_index("img")
        self.core = self.img % 2
        self.z = lax.axis_index("strip")
        self.host = self.z // group == self.core

    def flat(self, img, z):
        return img * self.strips + z

    def swap_core(self, values):
        return lax.ppermute(values, "img", [(i, i ^ 1) for i in range(self.images)])

    def across_img(self, values, bit):
        return lax.ppermute(values, "img", [(i, i ^ bit) for i in range(self.images)])

    def along_z(self, values, r):
        return lax.ppermute(values, "strip", [(z, z ^ r) for z in range(self.strips)])

    def route(self, r, back):
        pairs = [
            (self.flat(i, z), self.flat(i, z ^ r))
            for i in range(self.images)
            for z in range(self.strips)
            if (z ^ r) // self.group == i % 2
        ]
        return [(b, a) for a, b in pairs] if back else pairs

    def half(self, to_host):
        return [
            (self.flat(i, z), self.flat(i ^ 1, z))
            for i in range(self.images)
            for z in range(self.strips)
            if (z // self.group == i % 2) != to_host
        ]


def pick(values, index, axis=0):
    return lax.dynamic_index_in_dim(values, index, axis, keepdims=False)


def to_image(place, values, starts):
    group, capacity, grid, width = values.shape
    blocks = [pick(values, place.z % group)]
    for r in range(1, place.strips):
        send = pick(values, (place.z ^ r) % group)
        blocks.append(lax.ppermute(send, AXES, place.route(r, False)))
    stacked = jnp.stack(blocks)
    rows = jnp.zeros((grid + capacity, grid, width), values.dtype)
    for j in range(place.strips):
        rows = lax.dynamic_update_slice(rows, pick(stacked, place.z ^ j), (starts[j], 0, 0))
    half = grid // 2
    kept = lax.dynamic_slice_in_dim(rows, place.core * half, half, 0)
    sent = lax.dynamic_slice_in_dim(rows, (1 - place.core) * half, half, 0)
    received = lax.ppermute(sent, AXES, place.half(False))
    return jnp.where(place.host, kept, received).reshape(half * grid, width)


def to_strips(place, values, starts, capacity, grid):
    tokens, width = values.shape
    received = lax.ppermute(values, AXES, place.half(True))
    low = jnp.where(place.core == 0, values, received)
    high = jnp.where(place.core == 0, received, values)
    pad = jnp.zeros((capacity, grid, width), values.dtype)
    rows = jnp.concatenate(
        [low.reshape(-1, grid, width), high.reshape(-1, grid, width), pad], axis=0
    )
    pieces = []
    for r in range(place.strips):
        piece = lax.dynamic_slice(
            rows, (pick(starts, place.z ^ r), 0, 0), (capacity, grid, width)
        )
        if r:
            piece = lax.ppermute(piece, AXES, place.route(r, True))
        pieces.append(piece)
    out = []
    for g in range(place.group):
        owner = (place.img % 2) * place.group + g
        block = pieces[0]
        for r in range(1, place.strips):
            block = jnp.where(place.z ^ r == owner, pieces[r], block)
        out.append(block)
    return jnp.stack(out)


def scatter_sum(place, grad, low):
    f32 = jnp.float32
    width = grad.shape[-1]
    hi = place.images // 2
    grad = grad.reshape(hi, 2, -1, width)
    send = pick(grad, 1 - place.core, 1).astype(low)
    total = pick(grad, place.core, 1).astype(f32) + place.swap_core(send).astype(f32)
    bits = []
    bit = 2
    while bit < place.images:
        bits.append(bit)
        bit *= 2
    cuts = len(bits) if width % (128 * len(bits)) == 0 else 1
    done = []
    for cut in range(cuts):
        part = total[..., cut * (width // cuts) : (cut + 1) * (width // cuts)]
        part = part.reshape((2,) * len(bits) + part.shape[1:])
        axes = list(reversed(bits))
        order = bits[cut:] + bits[:cut]
        for bit in order:
            axis = axes.index(bit)
            mine = (place.img // bit) % 2
            sent = pick(part, 1 - mine, axis).astype(low)
            part = pick(part, mine, axis) + place.across_img(sent, bit).astype(f32)
            axes.pop(axis)
        part = part.reshape(place.strips, -1, width // cuts)
        mine = pick(part, place.z)
        for r in range(1, place.strips):
            sent = pick(part, place.z ^ r).astype(low)
            mine = mine + place.along_z(sent, r).astype(f32)
        done.append(mine)
    return jnp.concatenate(done, axis=-1)


def body(
    pixels,
    cotangent,
    resize,
    patch_index,
    slot_image,
    strip_rows,
    patch_weight,
    pos_grid,
    patch_bias,
    attention_norm_gain,
    attn_shift,
    query_weight,
    query_bias,
    key_weight,
    value_weight,
    value_bias,
    out_weight,
    out_bias,
    mlp_gain,
    mlp_shift,
    up_weight,
    up_bias,
    down_weight,
    down_bias,
):
    group, capacity, grid, pixel_len = pixels.shape
    width = cotangent.shape[3]
    ff = up_weight.shape[1]
    local_rows = capacity * grid
    tokens = group * local_rows
    f32 = jnp.float32
    bf16 = jnp.bfloat16
    place = Place(group)
    devices = place.images * place.strips
    first_slot = place.img * group
    shard = patch_bias.shape[0]

    vectors = (
        patch_bias,
        attention_norm_gain,
        attn_shift,
        query_bias,
        value_bias,
        out_bias,
        mlp_gain,
        mlp_shift,
        down_bias,
    )
    small = jnp.concatenate(vectors + (up_bias, pos_grid.reshape(-1)))
    pad = -small.shape[0] % width
    small = jnp.pad(small, (0, pad)).reshape(-1, width)
    small_rows = small.shape[0]
    extra = 16 * (-(-small_rows // 16))
    small = jnp.pad(small, ((0, extra - small_rows), (0, 0)))
    w_patch = lax.all_gather(patch_weight, AXES, axis=0, tiled=True)
    packed = lax.all_gather(
        jnp.concatenate([query_weight, key_weight, value_weight, out_weight, small]), AXES, axis=0
    )
    w_up = lax.all_gather(up_weight, AXES, axis=0, tiled=True)
    w_down = lax.all_gather(down_weight, AXES, axis=0, tiled=True)
    w_query, w_key, w_value, w_out = (
        packed[:, i * shard : (i + 1) * shard].reshape(width, width) for i in range(4)
    )
    flat_small = packed[:, 4 * shard :].reshape(devices, -1)
    full_vectors = [
        flat_small[:, i * shard : (i + 1) * shard].reshape(1, width).astype(f32)
        for i in range(len(vectors))
    ]
    b_patch, g_one, c_one, b_query, b_value, b_out, g_two, c_two, b_down = full_vectors
    at = len(vectors) * shard
    ups = up_bias.shape[0]
    b_up = flat_small[:, at : at + ups].reshape(1, ff).astype(f32)
    at += ups
    grid_pos = (
        flat_small[:, at : at + BASE * BASE * shard]
        .reshape(devices, BASE * BASE, shard)
        .transpose(1, 0, 2)
        .reshape(BASE * BASE, width)
        .astype(f32)
    )

    size_count = resize.shape[0]
    side = resize.shape[1]
    step_px = side // size_count
    slot_ids = lax.dynamic_slice_in_dim(slot_image, first_slot, group)
    picked = slot_ids[:, None] == jnp.arange(patch_index.shape[0], dtype=jnp.int32)[None, :]
    size_index = jnp.sum(jnp.where(picked, patch_index[None, :], 0), axis=1)
    limit = step_px * (size_index + 1)
    tables = jnp.stack([pick(resize, size_index[g]) for g in range(group)])
    tables = jnp.where(
        jnp.arange(side, dtype=jnp.int32)[None, :, None] < limit[:, None, None], tables, 0.0
    )
    wide_rows = jnp.repeat(tables, side, axis=2)
    wide_columns = jnp.tile(tables, (1, 1, side))
    mixers = (
        (wide_rows[:, :, None, :] * wide_columns[:, None, :, :])
        .reshape(group, side * side, side * side)
        .astype(bf16)
    )
    counts = lax.dynamic_slice_in_dim(strip_rows, first_slot, group, 0)
    row_iota = jnp.arange(capacity, dtype=jnp.int32)
    live = row_iota[None, :] < pick(counts, place.z, 1)[:, None]
    token_live = jnp.broadcast_to(live[:, :, None, None], (group, capacity, grid, 1))
    image_counts = pick(strip_rows, (place.img // 2) * 2 * group + place.z)
    starts = jnp.cumsum(image_counts) - image_counts

    pix = pixels.reshape(group, local_rows, 3, side * side)
    base = [
        jnp.einsum(
            "gtj,gjk->gtk", pix[:, :, c], mixers, preferred_element_type=f32
        ).astype(bf16)
        for c in range(3)
    ]
    base_pixels = jnp.concatenate(base, axis=-1).reshape(tokens, pixel_len)
    patches = matmul(base_pixels, w_patch).astype(bf16)
    patches = to_image(place, patches.reshape(group, capacity, grid, width), starts).astype(f32)
    g_out_low = to_image(place, cotangent, starts)

    half = grid // 2
    spread = bilinear(grid, BASE)
    spread_all = jnp.asarray((spread[:, None, :, None] * spread[None, :, None, :]).reshape(2, half * grid, BASE * BASE))
    spread_here = pick(spread_all, place.core)
    place_rows = jnp.dot(spread_here, grid_pos, precision=HIGH_ACCURACY)
    embed = patches + b_patch + place_rows
    normed_one, norm_one_back = jax.vjp(layer_norm, embed, g_one, c_one)
    attn_in = normed_one.astype(bf16)
    query = ((matmul(attn_in, w_query) + b_query) * 0.125).astype(bf16)
    key = matmul(attn_in, w_key).astype(bf16)
    value = (matmul(attn_in, w_value) + b_value).astype(bf16)
    rows = query.shape[0]
    size = width // HEADS

    def split(values):
        return values.reshape(-1, HEADS, size).transpose(1, 0, 2)

    def join(values):
        return values.transpose(1, 0, 2).reshape(-1, width)

    keys = jnp.concatenate([key, place.swap_core(key)], axis=0)
    values = jnp.concatenate([value, place.swap_core(value)], axis=0)
    q_heads, k_heads, v_heads = split(query), split(keys), split(values)
    scores = jnp.einsum("hqd,hkd->hqk", q_heads, k_heads, preferred_element_type=f32)
    peak = jnp.max(scores, axis=-1, keepdims=True)
    expd = jnp.exp(scores - peak)
    denom = jnp.sum(expd, axis=-1, keepdims=True)
    probs = expd / denom
    probs_low = probs.astype(bf16)
    attended = join(
        jnp.einsum("hqk,hkd->hqd", probs_low, v_heads, preferred_element_type=f32).astype(bf16)
    )
    resid = embed + matmul(attended, w_out) + b_out
    normed_two, norm_two_back = jax.vjp(layer_norm, resid, g_two, c_two)
    mlp_in = normed_two.astype(bf16)
    upper = matmul(mlp_in, w_up) + b_up
    activ, gelu_back = jax.vjp(gelu_exact, upper)
    hidden = activ.astype(bf16)
    final = (resid + matmul(hidden, w_down) + b_down).astype(bf16)
    block_out = to_strips(place, final, starts, capacity, grid)
    block_out = jnp.where(token_live, block_out, 0.0)

    def column_sum(values):
        return jnp.sum(values, axis=0)

    g_out = g_out_low.astype(f32)
    grad_down_bias = column_sum(g_out)
    grad_down_weight = left_trans(hidden, g_out_low).astype(bf16)
    down_sum = scatter_sum(place, grad_down_weight, bf16)
    (g_upper,) = gelu_back(right_trans(g_out_low, w_down))
    grad_up_bias = column_sum(g_upper)
    g_upper_low = g_upper.astype(bf16)
    grad_up_weight = left_trans(mlp_in, g_upper_low).astype(bf16)
    up_sum = scatter_sum(place, grad_up_weight, bf16)
    g_resid_norm, grad_mlp_gain, grad_mlp_shift = norm_two_back(right_trans(g_upper_low, w_up))
    g_resid = g_out + g_resid_norm
    grad_out_bias = column_sum(g_resid)
    g_resid_low = g_resid.astype(bf16)
    grad_out_weight = left_trans(attended, g_resid_low).astype(bf16)
    g_att = split(right_trans(g_resid_low, w_out).astype(bf16))

    g_probs = jnp.einsum("hqd,hkd->hqk", g_att, v_heads, preferred_element_type=f32)
    inner = jnp.sum(probs * g_probs, axis=-1, keepdims=True)
    g_scores = (probs * (g_probs - inner)).astype(bf16)
    g_query = join(jnp.einsum("hqk,hkd->hqd", g_scores, k_heads, preferred_element_type=f32))
    g_keys = join(jnp.einsum("hqk,hqd->hkd", g_scores, q_heads, preferred_element_type=f32))
    g_values = join(jnp.einsum("hqk,hqd->hkd", probs_low, g_att, preferred_element_type=f32))
    g_key = g_keys[:rows] + place.swap_core(g_keys[rows:].astype(bf16)).astype(f32)
    g_value = g_values[:rows] + place.swap_core(g_values[rows:].astype(bf16)).astype(f32)
    g_key_low = g_key.astype(bf16)
    g_value_low = g_value.astype(bf16)
    g_qin = g_query.astype(bf16).astype(f32) * 0.125
    grad_query_bias = column_sum(g_qin)
    g_qin_low = g_qin.astype(bf16)
    grad_query_weight = left_trans(attn_in, g_qin_low).astype(bf16)
    grad_key_weight = left_trans(attn_in, g_key_low).astype(bf16)
    grad_value_weight = left_trans(attn_in, g_value_low).astype(bf16)
    grad_value_bias = column_sum(g_value_low.astype(f32))
    qkvo = jnp.concatenate(
        [
            w.reshape(devices, shard, width)
            for w in (grad_query_weight, grad_key_weight, grad_value_weight, grad_out_weight)
        ],
        axis=1,
    ).reshape(-1, width)
    qkvo_sum = scatter_sum(place, qkvo, bf16)
    g_norm_in = (
        right_trans(g_qin_low, w_query)
        + right_trans(g_key_low, w_key)
        + right_trans(g_value_low, w_value)
    )
    g_embed_norm, grad_attn_gain, grad_attn_shift = norm_one_back(g_norm_in)
    g_embed = g_resid + g_embed_norm
    grad_patch_bias = column_sum(g_embed)
    grad_pos = lax.dot_general(
        spread_here, g_embed, (((0,), (0,)), ((), ())), precision=HIGH_ACCURACY
    )
    back = to_strips(place, g_embed.astype(bf16), starts, capacity, grid)
    g_embed_low = jnp.where(token_live, back, 0.0).reshape(tokens, width)
    grad_patch_weight = left_trans(base_pixels, g_embed_low).astype(bf16)
    patch_sum = scatter_sum(place, grad_patch_weight, bf16)

    pieces = [
        g.reshape(devices, shard)
        for g in (
            grad_patch_bias,
            grad_attn_gain,
            grad_attn_shift,
            grad_query_bias,
            grad_value_bias,
            grad_out_bias,
            grad_mlp_gain,
            grad_mlp_shift,
            grad_down_bias,
        )
    ]
    pieces.append(grad_up_bias.reshape(devices, ups))
    pieces.append(
        grad_pos.reshape(BASE * BASE, devices, shard).transpose(1, 0, 2).reshape(devices, -1)
    )
    small_grads = jnp.concatenate(pieces, axis=1)
    small_grads = jnp.pad(small_grads, ((0, 0), (0, pad))).reshape(devices * small_rows, width)
    small_sum = scatter_sum(place, small_grads, f32).reshape(-1)

    g_base = right_trans(g_embed_low, w_patch).astype(bf16).reshape(group, local_rows, pixel_len)
    wide = side * side
    pixel_grad = jnp.concatenate(
        [
            jnp.einsum(
                "gtk,gjk->gtj",
                g_base[:, :, c * wide : (c + 1) * wide],
                mixers,
                preferred_element_type=f32,
            )
            for c in range(3)
        ],
        axis=-1,
    ).reshape(pixels.shape)

    sums = [small_sum[i * shard : (i + 1) * shard] for i in range(len(vectors))]
    at = len(vectors) * shard
    s_up_bias = small_sum[at : at + ups]
    at += ups
    s_pos = small_sum[at : at + BASE * BASE * shard].reshape(BASE * BASE, shard)
    s_query, s_key, s_value, s_out = (qkvo_sum[i * shard : (i + 1) * shard] for i in range(4))
    return (
        block_out,
        pixel_grad,
        patch_sum,
        s_pos,
        sums[0],
        sums[1],
        sums[2],
        s_query,
        sums[3],
        s_key,
        s_value,
        sums[4],
        s_out,
        sums[5],
        sums[6],
        sums[7],
        up_sum,
        s_up_bias,
        down_sum,
        sums[8],
    )


def solution(mesh):
    rows = P(("img", "strip"))
    split_rows = P(("img", "strip"), None)
    split_columns = P(None, ("img", "strip"))
    held = P("img", "strip", None, None)
    return jax.shard_map(
        body,
        mesh=mesh,
        in_specs=(
            held,
            held,
            P(),
            P(),
            P(),
            P(),
            split_rows,
            split_columns,
            rows,
            rows,
            rows,
            split_rows,
            rows,
            split_rows,
            split_rows,
            rows,
            split_rows,
            rows,
            rows,
            rows,
            split_rows,
            rows,
            split_rows,
            rows,
        ),
        out_specs=(
            held,
            held,
            split_rows,
            split_columns,
            rows,
            rows,
            rows,
            split_rows,
            rows,
            split_rows,
            split_rows,
            rows,
            split_rows,
            rows,
            rows,
            rows,
            split_rows,
            rows,
            split_rows,
            rows,
        ),
        check_vma=False,
    )
```

time: 2000 us -> 723 us (0.36)
  waiting for transfers between devices: 1150 us -> 150 us
  matrix products: 351 us -> 159 us
  blocking collectives: 153 us -> 0 us
  local copies, waits for them, and re-layouts: 262 us -> 125 us
  starting transfers between devices: 1.55 us -> 126 us
  other arithmetic: 56.1 us -> 91.4 us
  Pallas kernels: 0 us -> 28.1 us
  between operations: 14.9 us -> 35.6 us
    reduce_scatter x7 -> x0, waiting for transfers between devices: 752 us -> none  [the longest x1 142 us: body(): lax.psum_scatter(grad_down_weight, ('img', 'strip'), scatter_dimension=0,...]
    all_gather x9 -> x4, waiting for transfers between devices: 252 us -> 39 us  [the longest x1 37.9 us: body(): w_down = lax.all_gather(down_weight, AXES, axis=0, tiled=True)]
    unnamed x22 -> x4, waiting for transfers between devices: 146 us -> 1.4 us
    dot_general x92 -> x12, matrix products: 211 us -> 66.4 us  [the longest x1 17.7 us: body(): jnp.einsum('hqd,hkd->hqk', g_att, v_heads, preferred_element_type=f32)]
    ppermute x0 -> x75, starting transfers between devices: none -> 126 us  [the longest x30 54.9 us: along_z(): lax.ppermute(values, 'strip', [(z, z ^ r) for z in range(self.strips)])]
    ppermute x0 -> x75, waiting for transfers between devices: none -> 109 us  [the longest x20 43.8 us: across_img(): lax.ppermute(values, 'img', [(i, i ^ bit) for i in range(self.images)])]
    unnamed x2 -> x0, blocking collectives: 84.9 us -> none
    unnamed x141 -> x159, local copies, waits for them, and re-layouts: 92.9 us -> 14.8 us
  transfers between devices with their start and end apart: 19 -> 79, of which waited for: 14 -> 30; matrix products, arithmetic and copies ran while one was open for 22% -> 34% of each run, Pallas kernels for 0% -> 4%
where the time goes in v1:
time: 723 us; the launch traced here: 715 us
  matrix products  159 us (22%)
  waiting for transfers between devices  150 us (21%)
  starting transfers between devices  126 us (17%)
  local copies, waits for them, and re-layouts  125 us (17%)
  other arithmetic  91.4 us (13%)
  between operations  35.6 us (5%)
  Pallas kernels  28.1 us (4%)
    ppermute x30, starting transfers between devices, along_z(): lax.ppermute(values, 'strip', [(z, z ^ r) for z in range(self.strips)])  54.9 us
    ppermute x20, waiting for transfers between devices, across_img(): lax.ppermute(values, 'img', [(i, i ^ bit) for i in range(self.images)])  43.8 us
    all_gather x1, waiting for transfers between devices, body(): w_down = lax.all_gather(down_weight, AXES, axis=0, tiled=True)  37.9 us
    dot_general x7, matrix products, right_trans(): lax.dot_general(left, right, (((1,), (1,)), ((), ())), preferred_element_...  33.1 us
    dot_general x1, Pallas kernels, body(): jnp.einsum('hqk,hkd->hqd', probs_low, v_heads, preferred_element_type=f32)  28.1 us
    dot_general x7, matrix products, matmul(): return jnp.dot(left, right, preferred_element_type=jnp.float32)  27.3 us
    ppermute x6, waiting for transfers between devices, to_image(): blocks.append(lax.ppermute(send, AXES, place.route(r, False)))  26 us
    ppermute x20, starting transfers between devices, across_img(): lax.ppermute(values, 'img', [(i, i ^ bit) for i in range(self.images)])  23.5 us
  transfers between devices with their start and end apart: 79, of which 30 were waited for; matrix products, arithmetic and copies ran while one was open for 34% of the time, Pallas kernels for 4%

profile of v1, /device:TPU:0, one launch (start us, length us, event | category | flops | bytes accessed | tf_op | source)
XLA Modules:
  0.0 715.5 jit_solution(17566413435686488955)
XLA Ops:
  8.9 6.8 concatenate.50
  37.6 13.7 %reshape.593 = bf16[2,384,3,1024]{3,2,1,0:T(4,128)(2,1)} reshape(bf16[2,12,32,3072]{3,2,1,0:T(8,128)(2,1)} %param.25) | data formatting | bytes 9437184 | tf_op jit(solution)/shard_map/reshape | solution.py:276
  51.3 14.1 %fusion.141 = (bf16[2,384,1,1024]{3,2,1,0:T(2,128)(2,1)S(1)}, bf16[2,384,1,1024]{3,2,1,0:T(2,128)(2,1)S(1)}, bf16[2,384,1,1024]{3,2,1,0:T(2,128)(2,1)S(1)}) fusion(bf16[2,384,3,1024]{3,2,1,0:T(4,128)(2,1)} %reshape.593), kind=kLoop, calls=%fused_computation.376 | loop fusion | bytes 9437184 | tf_op jit(solution)/shard_map/slice | solution.py:279
  78.4 6.9 copy.122
  85.4 7.6 %convolution_convert_fusion.11 = bf16[768,768]{1,0:T(8,128)(2,1)S(1)} fusion(bf16[768,3072]{1,0:T(8,128)(2,1)} %bitcast.538, bf16[3072,768]{1,0:T(8,128)(2,1)} %all-gather.6.cloned.1.call-done), kind=kOutput, calls=%fused_computation.102 | convolution fusion | flops 3624468480 | bytes 10616832 | tf_op jit(solution)/shard_map/dot_general | solution.py:31
  110.9 7.8 %collective-permute-done.2 = bf16[12,32,768]{2,1,0:T(8,128)(2,1)} collective-permute-done((bf16[12,32,768]{2,1,0:T(8,128)(2,1)}, bf16[12,32,768]{2,1,0:T(8,128)(2,1)}, u32[]{:S(2)}, u32[]{:S(2)}) %collective-permute-start.2) | collective-permute-done | bytes 589856 | tf_op jit(solution)/shard_map/ppermute | solution.py:96
  118.7 18.2 %collective-permute-done.1 = bf16[12,32,768]{2,1,0:T(8,128)(2,1)} collective-permute-done((bf16[12,32,768]{2,1,0:T(8,128)(2,1)}, bf16[12,32,768]{2,1,0:T(8,128)(2,1)}, u32[]{:S(2)}, u32[]{:S(2)}) %collective-permute-start.1) | collective-permute-done | bytes 589856 | tf_op jit(solution)/shard_map/ppermute | solution.py:96
  206.7 28.1 %dot_general.146 = f32[12,512,64]{2,1,0:T(8,128)} custom-call(bf16[12,512,64]{2,1,0:T(8,128)(2,1)} %bitcast.532, bf16[12,1024,64]{2,1,0:T(8,128)(2,1)} %bitcast.511, bf16[12,1024,64]{2,1,0:T(8,128)(2,1)} %bitcast.510), custom_call_target="tpu_custom_call" | custom-call | flops 1610612736 | bytes 3932160 | tf_op jit(solution)/shard_map/hqk,hkd->hqd/dot_general | solution.py:318
  244.5 8.3 %fusion.129 = f32[512,3072]{1,0:T(8,128)} fusion(bf16[768,3072]{1,0:T(8,128)(2,1)} %all-gather.8.cloned.1.call-done, f32[512,768]{1,0:T(8,128)} %copy-done.14, f32[768]{0:T(1024)S(1)} %copy-done.55, f32[768]{0:T(1024)S(1)} %copy-done.52, f32[512]{0:T(512)S(1)} %fusion.127, f32[512]{0:T(512)S(1)} %broadcast_multiply_fusion), kind=kOutput, calls=%fused_computation.370 | convolution fusion | flops 2417885184 | bytes 12593152 | tf_op jit(solution)/shard_map/dot_general | solution.py:31
  252.8 37.9 %all-gather.10.cloned.1.call-done = bf16[3072,768]{1,0:T(8,128)(2,1)} async-done(((bf16[96,768]{1,0:T(8,128)(2,1)}), bf16[3072,768]{1,0:T(8,128)(2,1)}) %all-gather.10.cloned.1.call-update) | async-done | bytes 4718608 | tf_op jit(solution)/shard_map/all_gather | solution.py:229
  290.7 19.9 %fusion.134 = (f32[3072]{0:T(1024)S(1)}, bf16[512,3072]{1,0:T(8,128)(2,1)S(1)}, f32[512,3072]{1,0:T(8,128)}) fusion(f32[512,3072]{1,0:T(8,128)} %fusion.129, f32[3072]{0:T(1024)S(1)} %reshape.667, bf16[512,768]{1,0:T(8,128)(2,1)S(1)} %bitcast.564, bf16[3072,768]{1,0:T(8,128)(2,1)} %all-gather.10.cloned.1.call-done), kind=kOutput, calls=%fused_computation.371 | convolution fusion | flops 2532307968 | bytes 21258240 | tf_op jit(solution)/shard_map/dot_general | solution.py:41
  325.4 11.4 %fusion.153 = (f32[12,512]{1,0:T(8,128)S(1)}, f32[12,512,1024]{2,1,0:T(8,128)}) fusion(bf16[12,512,64]{1,2,0:T(8,128)(2,1)S(1)} %bitcast.503, bf16[12,1024,64]{1,2,0:T(8,128)(2,1)S(1)} %bitcast.498), kind=kOutput, calls=%fused_computation.388 | convolution fusion | flops 817890304 | bytes 27549696 | tf_op jit(solution)/shard_map/sub | solution.py:313
  336.8 9.0 %fusion.11 = f32[1024,12,64]{0,2,1:T(8,128)} fusion(bf16[12,512,64]{1,2,0:T(8,128)(2,1)S(1)} %bitcast.602, f32[12,512]{1,0:T(8,128)S(1)} %get-tuple-element.216, bf16[12,512,64]{1,2,0:T(8,128)(2,1)S(1)} %bitcast.504, bf16[12,1024,64]{1,2,0:T(8,128)(2,1)S(1)} %bitcast.499), kind=kOutput, calls=%fused_computation.48 | convolution fusion | flops 1629494272 | bytes 6316032 | tf_op jit(solution)/shard_map/hqk,hqd->hkd/dot_general | solution.py:354
  345.7 17.7 %multiply_reduce_fusion = (f32[12,512]{1,0:T(8,128)S(1)}, f32[12,512,1024]{2,1,0:T(8,128)}) fusion(f32[12,512,1024]{2,1,0:T(8,128)} %get-tuple-element.217, f32[12,512]{1,0:T(8,128)S(1)} %get-tuple-element.216, bf16[12,512,64]{1,2,0:T(8,128)(2,1)S(1)} %bitcast.603, bf16[12,1024,64]{1,2,0:T(8,128)(2,1)} %bitcast.531), kind=kOutput, calls=%fused_computation.2 | convolution fusion | flops 824174592 | bytes 52740096 | tf_op jit(solution)/shard_map/hqd,hkd->hqk/dot_general | solution.py:349
  363.4 21.4 %multiply_convert_fusion = bf16[12,512,1024]{2,1,0:T(8,128)(2,1)} fusion(f32[12,512,1024]{2,1,0:T(8,128)} %get-tuple-element.219, f32[12,512]{1,0:T(8,128)S(1)} %get-tuple-element.218, f32[12,512,1024]{2,1,0:T(8,128)} %get-tuple-element.217, f32[12,512]{1,0:T(8,128)S(1)} %get-tuple-element.216), kind=kLoop, calls=%fused_computation.1 | loop fusion | flops 25165824 | bytes 62963712 | tf_op jit(solution)/shard_map/convert_element_type | solution.py:351
  384.8 9.9 %fusion.25 = (bf16[12,512,64]{1,2,0:T(8,128)(2,1)}, bf16[512,12,64]{0,2,1:T(8,128)(2,1)}, bf16[12,512,64]{1,2,0:T(8,128)(2,1)}) fusion(bf16[12,512,1024]{2,1,0:T(8,128)(2,1)} %multiply_convert_fusion, bf16[12,1024,64]{1,2,0:T(8,128)(2,1)S(1)} %bitcast.500), kind=kOutput, calls=%fused_computation.83 | convolution fusion | flops 807272448 | bytes 16515072 | tf_op jit(solution)/shard_map/hqk,hkd->hqd/dot_general | solution.py:352
  394.8 6.9 convolution_bitcast_fusion
  401.7 7.3 %multiply_convert_fusion.2 = bf16[512,3072]{1,0:T(8,128)(2,1)S(1)} fusion(f32[512,3072]{1,0:T(8,128)} %get-tuple-element.88, f32[512,3072]{1,0:T(8,128)} %fusion.129, f32[3072]{0:T(1024)S(1)} %reshape.667), kind=kLoop, calls=%fused_computation.12 | loop fusion | flops 6291456 | bytes 15740928 | tf_op jit(solution)/shard_map/convert_element_type | solution.py:325
  517.7 6.4 collective-permute-done.8
  558.2 7.6 %pad_maximum_fusion = f32[2,384,3072]{2,1,0:T(8,128)} fusion(f32[2,384,1024]{2,1,0:T(8,128)S(1)} %fusion.14, f32[2,384,1024]{2,1,0:T(8,128)} %fusion.16, f32[2,384,1024]{2,1,0:T(8,128)} %fusion.18), kind=kLoop, calls=%fused_computation.8 | loop fusion | flops 4718592 | bytes 18874368 | tf_op jit(solution)/shard_map/concatenate | solution.py:414
  576.2 9.8 %collective-permute-done.54 = bf16[2,96,1536]{2,1,0:T(8,128)(2,1)S(1)} collective-permute-done((bf16[2,96,1536]{2,1,0:T(8,128)(2,1)S(1)}, bf16[2,96,1536]{2,1,0:T(8,128)(2,1)S(1)}, u32[]{:S(2)}, u32[]{:S(2)}) %collective-permute-start.54) | collective-permute-done | bytes 589856 | tf_op jit(solution)/shard_map/ppermute | solution.py:64
  588.4 9.2 %collective-permute-done.65 = bf16[2,384,384]{2,1,0:T(8,128)(2,1)S(1)} collective-permute-done((bf16[2,384,384]{2,1,0:T(8,128)(2,1)S(1)}, bf16[2,384,384]{2,1,0:T(8,128)(2,1)S(1)}, u32[]{:S(2)}, u32[]{:S(2)}) %collective-permute-start.65) | collective-permute-done | bytes 589856 | tf_op jit(solution)/shard_map/ppermute | solution.py:64
  610.1 10.1 %collective-permute-start.56 = (bf16[24,1536]{1,0:T(8,128)(2,1)S(1)}, bf16[24,1536]{1,0:T(8,128)(2,1)S(1)}, u32[]{:S(2)}, u32[]{:S(2)}) collective-permute-start(bf16[24,1536]{1,0:T(8,128)(2,1)S(1)} %get-tuple-element.157), channel_id=1, source_target_pairs={{0,1},{1,0},{2,3},{3,2},{4,5},{5,4},{6,7},{7,6},{8,9},{9,8},{10,11... | collective-permute-start | bytes 221192 | tf_op jit(solution)/shard_map/ppermute | solution.py:67
  679.5 7.1 collective-permute-done.21
  (556 shorter events, 377.1 us)
Async XLA Ops:
  7.2 78.1 %all-gather.6.cloned.1.call-start = ((), (), s32[]{:S(2)}) async-start(), calls=%async_computation | async-start | bytes 4866048 | tf_op jit(solution)/shard_map/all_gather | solution.py:224
  7.9 152.8 %all-gather.12.cloned.1.call-start = ((), (), s32[]{:S(2)}) async-start(), calls=%async_computation.3 | async-start | bytes 5677056 | tf_op jit(solution)/shard_map/all_gather | solution.py:225
  19.5 225.0 %all-gather.8.cloned.1.call-start = ((), (), s32[]{:S(2)}) async-start(), calls=%async_computation.1 | async-start | bytes 4866048 | tf_op jit(solution)/shard_map/all_gather | solution.py:228
  20.2 270.5 %all-gather.10.cloned.1.call-start = ((), (), s32[]{:S(2)}) async-start(), calls=%async_computation.2 | async-start | bytes 4866048 | tf_op jit(solution)/shard_map/all_gather | solution.py:229
  23.3 73.5 %collective-permute-start.10 = (bf16[12,32,768]{2,1,0:T(8,128)(2,1)}, bf16[12,32,768]{2,1,0:T(8,128)(2,1)S(1)}, u32[]{:S(2)}, u32[]{:S(2)}) collective-permute-start(bf16[12,32,768]{2,1,0:T(8,128)(2,1)} %get-tuple-element.133), channel_id=1, source_target_pairs={{0,1},{1,0},{6,7},{7,6},{8,9},{9,8},{14,15},{15,14},{16,17},{17,16... | collective-permute-start | bytes 1769480 | tf_op jit(solution)/shard_map/ppermute | solution.py:96
  28.3 80.5 %collective-permute-start.12 = (bf16[12,32,768]{2,1,0:T(8,128)(2,1)}, bf16[12,32,768]{2,1,0:T(8,128)(2,1)}, u32[]{:S(2)}, u32[]{:S(2)}) collective-permute-start(bf16[12,32,768]{2,1,0:T(8,128)(2,1)} %get-tuple-element.134), channel_id=1, source_target_pairs={{2,1},{3,0},{4,7},{5,6},{10,9},{11,8},{12,15},{13,14},{18,17},{19,... | collective-permute-start | bytes 1769480 | tf_op jit(solution)/shard_map/ppermute | solution.py:96
  29.6 79.2 %collective-permute-start.11 = (bf16[12,32,768]{2,1,0:T(8,128)(2,1)}, bf16[12,32,768]{2,1,0:T(8,128)(2,1)}, u32[]{:S(2)}, u32[]{:S(2)}) collective-permute-start(bf16[12,32,768]{2,1,0:T(8,128)(2,1)} %get-tuple-element.135), channel_id=1, source_target_pairs={{2,0},{3,1},{4,6},{5,7},{10,8},{11,9},{12,14},{13,15},{18,16},{19,... | collective-permute-start | bytes 1769480 | tf_op jit(solution)/shard_map/ppermute | solution.py:96
  94.2 24.5 %collective-permute-start.2 = (bf16[12,32,768]{2,1,0:T(8,128)(2,1)}, bf16[12,32,768]{2,1,0:T(8,128)(2,1)}, u32[]{:S(2)}, u32[]{:S(2)}) collective-permute-start(bf16[12,32,768]{2,1,0:T(8,128)(2,1)} %get-tuple-element.137), channel_id=1, source_target_pairs={{2,1},{3,0},{4,7},{5,6},{10,9},{11,8},{12,15},{13,14},{18,17},{19,... | collective-permute-start | bytes 1769480 | tf_op jit(solution)/shard_map/ppermute | solution.py:96
  95.5 41.4 %collective-permute-start.1 = (bf16[12,32,768]{2,1,0:T(8,128)(2,1)}, bf16[12,32,768]{2,1,0:T(8,128)(2,1)}, u32[]{:S(2)}, u32[]{:S(2)}) collective-permute-start(bf16[12,32,768]{2,1,0:T(8,128)(2,1)} %get-tuple-element.138), channel_id=1, source_target_pairs={{2,0},{3,1},{4,6},{5,7},{10,8},{11,9},{12,14},{13,15},{18,16},{19,... | collective-permute-start | bytes 1769480 | tf_op jit(solution)/shard_map/ppermute | solution.py:96
  96.8 40.1 %collective-permute-start = (bf16[12,32,768]{2,1,0:T(8,128)(2,1)}, bf16[12,32,768]{2,1,0:T(8,128)(2,1)}, u32[]{:S(2)}, u32[]{:S(2)}) collective-permute-start(bf16[12,32,768]{2,1,0:T(8,128)(2,1)} %get-tuple-element.139), channel_id=1, source_target_pairs={{0,1},{1,0},{6,7},{7,6},{8,9},{9,8},{14,15},{15,14},{16,17},{17,16... | collective-permute-start | bytes 1769480 | tf_op jit(solution)/shard_map/ppermute | solution.py:96
  175.0 19.6 %collective-permute-start.5 = (bf16[512,768]{1,0:T(8,128)(2,1)}, bf16[512,768]{1,0:T(8,128)(2,1)}, u32[]{:S(2)}, u32[]{:S(2)}) collective-permute-start(bf16[512,768]{1,0:T(8,128)(2,1)} %add_convert_fusion.2), channel_id=1, source_target_pairs={{0,4},{4,0},{8,12},{12,8},{16,20},{20,16},{24,28},{28,24},{1,5},{5... | collective-permute-start | bytes 2359304 | tf_op jit(solution)/shard_map/ppermute | solution.py:61
  417.0 44.5 %collective-permute-start.6 = (bf16[512,768]{1,0:T(8,128)(2,1)}, bf16[512,768]{1,0:T(8,128)(2,1)}, u32[]{:S(2)}, u32[]{:S(2)}) collective-permute-start(bf16[512,768]{1,0:T(8,128)(2,1)} %add_convert_fusion), channel_id=1, source_target_pairs={{2,6},{3,7},{4,0},{5,1},{10,14},{11,15},{12,8},{13,9},{18,22},{19,... | collective-permute-start | bytes 2359304 | tf_op jit(solution)/shard_map/ppermute | solution.py:110
  449.9 31.0 %collective-permute-start.16 = (bf16[512,768]{1,0:T(8,128)(2,1)}, bf16[512,768]{1,0:T(8,128)(2,1)}, u32[]{:S(2)}, u32[]{:S(2)}) collective-permute-start(bf16[512,768]{1,0:T(8,128)(2,1)} %convert_element_type.729), channel_id=1, source_target_pairs={{2,6},{3,7},{4,0},{5,1},{10,14},{11,15},{12,8},{13,9},{18,22},{19,... | collective-permute-start | bytes 2359304 | tf_op jit(solution)/shard_map/ppermute | solution.py:110
  496.8 20.9 %collective-permute-start.9 = (bf16[12,32,768]{2,1,0:T(8,128)(2,1)}, bf16[12,32,768]{2,1,0:T(8,128)(2,1)}, u32[]{:S(2)}, u32[]{:S(2)}) collective-permute-start(bf16[12,32,768]{2,1,0:T(8,128)(2,1)} %get-tuple-element.123), channel_id=1, source_target_pairs={{1,0},{0,1},{7,6},{6,7},{9,8},{8,9},{15,14},{14,15},{17,16},{16,17... | collective-permute-start | bytes 1769480 | tf_op jit(solution)/shard_map/ppermute | solution.py:123
  498.7 25.3 %collective-permute-start.8 = (bf16[12,32,768]{2,1,0:T(8,128)(2,1)}, bf16[12,32,768]{2,1,0:T(8,128)(2,1)}, u32[]{:S(2)}, u32[]{:S(2)}) collective-permute-start(bf16[12,32,768]{2,1,0:T(8,128)(2,1)} %get-tuple-element.124), channel_id=1, source_target_pairs={{0,2},{1,3},{6,4},{7,5},{8,10},{9,11},{14,12},{15,13},{16,18},{17,... | collective-permute-start | bytes 1769480 | tf_op jit(solution)/shard_map/ppermute | solution.py:123
  502.4 27.9 %collective-permute-start.7 = (bf16[12,32,768]{2,1,0:T(8,128)(2,1)}, bf16[12,32,768]{2,1,0:T(8,128)(2,1)}, u32[]{:S(2)}, u32[]{:S(2)}) collective-permute-start(bf16[12,32,768]{2,1,0:T(8,128)(2,1)} %get-tuple-element.125), channel_id=1, source_target_pairs={{1,2},{0,3},{7,4},{6,5},{9,10},{8,11},{15,12},{14,13},{17,18},{16,... | collective-permute-start | bytes 1769480 | tf_op jit(solution)/shard_map/ppermute | solution.py:123
  506.6 59.2 %collective-permute-start.53 = (bf16[4,96,3072]{2,1,0:T(8,128)(2,1)}, bf16[4,96,3072]{2,1,0:T(8,128)(2,1)}, u32[]{:S(2)}, u32[]{:S(2)}) collective-permute-start(bf16[4,96,3072]{2,1,0:T(8,128)(2,1)} %dynamic-slice_bitcast_fusion.1), channel_id=1, source_target_pairs={{0,4},{4,0},{8,12},{12,8},{16,20},{20,16},{24,28},{28,24},{1,5},{5... | collective-permute-start | bytes 7077896 | tf_op jit(solution)/shard_map/ppermute | solution.py:61
  511.2 60.7 %collective-permute-start.64 = (bf16[4,384,768]{2,1,0:T(8,128)(2,1)}, bf16[4,384,768]{2,1,0:T(8,128)(2,1)}, u32[]{:S(2)}, u32[]{:S(2)}) collective-permute-start(bf16[4,384,768]{2,1,0:T(8,128)(2,1)} %dynamic-slice_bitcast_fusion), channel_id=1, source_target_pairs={{0,4},{4,0},{8,12},{12,8},{16,20},{20,16},{24,28},{28,24},{1,5},{5... | collective-permute-start | bytes 7077896 | tf_op jit(solution)/shard_map/ppermute | solution.py:61
  517.7 86.2 %collective-permute-start.42 = (bf16[4,384,768]{2,1,0:T(8,128)(2,1)}, bf16[4,384,768]{2,1,0:T(8,128)(2,1)}, u32[]{:S(2)}, u32[]{:S(2)}) collective-permute-start(bf16[4,384,768]{2,1,0:T(8,128)(2,1)} %dynamic-slice_bitcast_fusion.2), channel_id=1, source_target_pairs={{0,4},{4,0},{8,12},{12,8},{16,20},{20,16},{24,28},{28,24},{1,5},{5... | collective-permute-start | bytes 7077896 | tf_op jit(solution)/shard_map/ppermute | solution.py:61
  540.6 127.7 %collective-permute-start.20 = (bf16[4,384,768]{2,1,0:T(8,128)(2,1)}, bf16[4,384,768]{2,1,0:T(8,128)(2,1)}, u32[]{:S(2)}, u32[]{:S(2)}) collective-permute-start(bf16[4,384,768]{2,1,0:T(8,128)(2,1)} %dynamic-slice_bitcast_fusion.3), channel_id=1, source_target_pairs={{0,4},{4,0},{8,12},{12,8},{16,20},{20,16},{24,28},{28,24},{1,5},{5... | collective-permute-start | bytes 7077896 | tf_op jit(solution)/shard_map/ppermute | solution.py:61
  574.5 23.1 %collective-permute-start.65 = (bf16[2,384,384]{2,1,0:T(8,128)(2,1)S(1)}, bf16[2,384,384]{2,1,0:T(8,128)(2,1)S(1)}, u32[]{:S(2)}, u32[]{:S(2)}) collective-permute-start(bf16[2,384,384]{2,1,0:T(8,128)(2,1)S(1)} %fusion.42), channel_id=1, source_target_pairs={{0,8},{4,12},{8,0},{12,4},{16,24},{20,28},{24,16},{28,20},{1,9},{5... | collective-permute-start | bytes 1769480 | tf_op jit(solution)/shard_map/ppermute | solution.py:64
  587.6 20.9 %collective-permute-start.55 = (bf16[96,1536]{1,0:T(8,128)(2,1)S(1)}, bf16[96,1536]{1,0:T(8,128)(2,1)S(1)}, u32[]{:S(2)}, u32[]{:S(2)}) collective-permute-start(bf16[96,1536]{1,0:T(8,128)(2,1)S(1)} %fusion.49), channel_id=1, source_target_pairs={{0,16},{4,20},{8,24},{12,28},{16,0},{20,4},{24,8},{28,12},{1,17},{... | collective-permute-start | bytes 884744 | tf_op jit(solution)/shard_map/ppermute | solution.py:64
  603.9 20.0 %collective-permute-start.71 = (bf16[384,384]{1,0:T(8,128)(2,1)S(1)}, bf16[384,384]{1,0:T(8,128)(2,1)S(1)}, u32[]{:S(2)}, u32[]{:S(2)}) collective-permute-start(bf16[384,384]{1,0:T(8,128)(2,1)S(1)} %fusion.52), channel_id=1, source_target_pairs={{0,8},{4,12},{8,0},{12,4},{16,24},{20,28},{24,16},{28,20},{1,9},{5... | collective-permute-start | bytes 884744 | tf_op jit(solution)/shard_map/ppermute | solution.py:64
  608.6 45.7 %collective-permute-start.48 = (bf16[2,384,384]{2,1,0:T(8,128)(2,1)S(1)}, bf16[2,384,384]{2,1,0:T(8,128)(2,1)S(1)}, u32[]{:S(2)}, u32[]{:S(2)}) collective-permute-start(bf16[2,384,384]{2,1,0:T(8,128)(2,1)S(1)} %fusion.37), channel_id=1, source_target_pairs={{0,16},{4,20},{8,24},{12,28},{16,0},{20,4},{24,8},{28,12},{1,17},{... | collective-permute-start | bytes 1769480 | tf_op jit(solution)/shard_map/ppermute | solution.py:64
  (133 other events, 1282.1 us)
Sparse Core Ops, SparseCore 0:
  10.8 74.1 all-gather.5
  88.4 72.2 all-gather.11
  163.6 62.0 all-gather.7
  228.3 62.3 all-gather.9

commit v2 on v1

v2 whole, which is shorter than its diff:
```python
import functools

import jax
import jax.numpy as jnp
import numpy as np
from jax import lax
from jax.experimental import pallas as pl
from jax.experimental.pallas import tpu as pltpu
from jax.sharding import PartitionSpec as P

HEADS = 12
BASE = 7
HIGH_ACCURACY = lax.Precision.HIGHEST
AXES = ("img", "strip")


def bilinear(out_count, in_count):
    source = (np.arange(out_count, dtype=np.float32) + 0.5) * (in_count / out_count) - 0.5
    source = np.clip(source, 0.0, in_count - 1.0)
    target = np.arange(in_count, dtype=np.float32)
    return np.maximum(1.0 - np.abs(source[:, None] - target[None, :]), 0.0).astype(np.float32)


def matmul(left, right):
    return jnp.dot(left, right, preferred_element_type=jnp.float32)


def left_trans(left, right):
    return lax.dot_general(
        left, right, (((0,), (0,)), ((), ())), preferred_element_type=jnp.float32
    )


def right_trans(left, right):
    return lax.dot_general(
        left, right, (((1,), (1,)), ((), ())), preferred_element_type=jnp.float32
    )


f32 = jnp.float32
bf16 = jnp.bfloat16
VMEM_LIMIT = 56 << 20


def params(*semantics):
    return pltpu.CompilerParams(
        dimension_semantics=semantics or None, vmem_limit_bytes=VMEM_LIMIT
    )


def shaped(shape, dtype):
    return jax.ShapeDtypeStruct(shape, dtype)


def cost(light=False):
    flops = 1024 if light else 1 << 32
    return pl.CostEstimate(flops=flops, bytes_accessed=1024, transcendentals=0)


def fill_mixer(mixer, table, size, turned):
    side = table.shape[0]
    span = side * side
    live = lax.broadcasted_iota(jnp.int32, table.shape, 0) < size
    table = jnp.where(live, table, 0.0)
    column = lax.broadcasted_iota(jnp.int32, (side, span), 1)
    row = lax.broadcasted_iota(jnp.int32, (side, span), 0)

    def widen(chosen):
        return lax.dot_general(
            table,
            chosen.astype(f32),
            (((0 if turned else 1,), (0,)), ((), ())),
            precision=HIGH_ACCURACY,
            preferred_element_type=f32,
        )

    wide = widen(column // side == row)
    tall = widen(column % side == row)
    for i in range(side):
        mixer[i * side : (i + 1) * side, :] = (wide[i : i + 1, :] * tall).astype(bf16)


def mix_kernel(sizes_ref, table_ref, pix_ref, out_ref, mixer):
    step = table_ref.shape[0] // sizes_ref[2]
    size = (sizes_ref[pl.program_id(0)] + 1) * step
    fill_mixer(mixer, table_ref[...], size, False)
    span = mixer.shape[0]
    for c in range(pix_ref.shape[-1] // span):
        columns = slice(c * span, (c + 1) * span)
        out_ref[:, columns] = matmul(pix_ref[:, columns], mixer[...]).astype(bf16)


def mix(sizes, resize, pixels):
    group, rows, length = pixels.shape
    side = resize.shape[1]
    span = side * side
    block = pl.BlockSpec((None, rows, length), lambda g, p: (g, 0, 0))
    return pl.pallas_call(
        mix_kernel,
        grid_spec=pltpu.PrefetchScalarGridSpec(
            num_scalar_prefetch=1,
            grid=(group,),
            in_specs=[pl.BlockSpec((None, side, side), lambda g, p: (p[g], 0, 0)), block],
            out_specs=block,
            scratch_shapes=[pltpu.VMEM((span, span), bf16)],
        ),
        out_shape=shaped(pixels.shape, bf16),
        compiler_params=params("arbitrary"),
        cost_estimate=cost(),
        name="mix",
    )(sizes, resize, pixels)


def unmix_kernel(sizes_ref, table_ref, left_ref, right_ref, grad_ref, out_ref, mixer):
    group = grad_ref.shape[0]

    @pl.when(pl.program_id(0) == 0)
    def _():
        step = table_ref.shape[1] // table_ref.shape[0]
        for g in range(group):
            index = sizes_ref[g]
            fill_mixer(mixer.at[g], table_ref[index], (index + 1) * step, True)

    half = left_ref.shape[1]
    for g in range(group):
        grad = grad_ref[g]
        g_base = (
            right_trans(grad[:, :half], left_ref[...]) + right_trans(grad[:, half:], right_ref[...])
        ).astype(bf16)
        out_ref[g] = matmul(g_base, mixer[g])


def unmix(sizes, resize, left, right, grad):
    group, rows, width = grad.shape
    side = resize.shape[1]
    span = side * side
    length, columns = left.shape
    return pl.pallas_call(
        unmix_kernel,
        grid_spec=pltpu.PrefetchScalarGridSpec(
            num_scalar_prefetch=1,
            grid=(length // span,),
            in_specs=[
                pl.BlockSpec(resize.shape, lambda c, p: (0, 0, 0)),
                pl.BlockSpec((span, columns), lambda c, p: (c, 0)),
                pl.BlockSpec((span, columns), lambda c, p: (c, 0)),
                pl.BlockSpec((group, rows, width), lambda c, p: (0, 0, 0)),
            ],
            out_specs=pl.BlockSpec((group, rows, span), lambda c, p: (0, 0, c)),
            scratch_shapes=[pltpu.VMEM((group, span, span), bf16)],
        ),
        out_shape=shaped((group, rows, length), f32),
        compiler_params=params("arbitrary"),
        cost_estimate=cost(),
        name="unmix",
    )(sizes, resize, left, right, grad)


def attend_kernel(q_ref, ko_ref, kp_ref, vo_ref, vp_ref, out_ref, lse_ref, *, size, chunk):
    first = lax.broadcasted_iota(jnp.int32, (1, 2 * size), 1) < size
    keys = jnp.concatenate([ko_ref[...], kp_ref[...]], axis=0)
    values = jnp.concatenate([vo_ref[...], vp_ref[...]], axis=0)
    for i in range(q_ref.shape[0] // chunk):
        rows = slice(i * chunk, (i + 1) * chunk)
        query = q_ref[rows, :]
        none = jnp.zeros_like(query)
        outs, sums = [], []
        for e in range(2):
            head = jnp.where(first, query, none) if e == 0 else jnp.where(first, none, query)
            scores = right_trans(head, keys)
            peak = jnp.max(scores, axis=-1, keepdims=True)
            expd = jnp.exp(scores - peak)
            denom = jnp.sum(expd, axis=-1, keepdims=True)
            outs.append(matmul(expd.astype(bf16), values) / denom)
            sums.append(peak + jnp.log(denom))
        out_ref[rows, :] = jnp.where(first, outs[0], outs[1]).astype(bf16)
        lse_ref[rows, :] = jnp.where(first, sums[0], sums[1])


def attend(query, key, key_peer, value, value_peer):
    rows, width = query.shape
    size = width // HEADS
    spec = pl.BlockSpec((rows, 2 * size), lambda h: (0, h))
    return pl.pallas_call(
        functools.partial(attend_kernel, size=size, chunk=min(256, rows)),
        grid=(HEADS // 2,),
        in_specs=[spec] * 5,
        out_specs=[spec] * 2,
        out_shape=[shaped((rows, width), bf16), shaped((rows, width), f32)],
        compiler_params=params("arbitrary"),
        cost_estimate=cost(),
        name="attend",
    )(query, key, key_peer, value, value_peer)


def attend_back_kernel(
    q_ref,
    ko_ref,
    kp_ref,
    vo_ref,
    vp_ref,
    g_ref,
    o_ref,
    lse_ref,
    gq_ref,
    gko_ref,
    gkp_ref,
    gvo_ref,
    gvp_ref,
    *,
    size,
    chunk,
):
    rows = q_ref.shape[0]
    upper = lax.broadcasted_iota(jnp.int32, (2 * size, 1), 0) < size
    first = lax.broadcasted_iota(jnp.int32, (1, 2 * size), 1) < size
    query = q_ref[...]
    grad = g_ref[...]
    query_t = query.astype(f32).T
    grad_t = grad.astype(f32).T
    inner_t = grad_t * o_ref[...].astype(f32).T
    lse_t = lse_ref[...].T
    queries, grads, inners, sums, g_query = [], [], [], [], []
    for e in range(2):
        mine = upper if e == 0 else jnp.logical_not(upper)
        queries.append(jnp.where(mine, query_t, 0.0).astype(bf16))
        grads.append(jnp.where(mine, grad_t, 0.0).astype(bf16))
        inners.append(jnp.sum(inner_t[e * size : (e + 1) * size], axis=0, keepdims=True))
        sums.append(lse_t[e * size : e * size + 1])
        g_query.append(jnp.zeros((size, rows), f32))
    for k_ref, v_ref, gk_ref, gv_ref in (
        (ko_ref, vo_ref, gko_ref, gvo_ref),
        (kp_ref, vp_ref, gkp_ref, gvp_ref),
    ):
        for i in range(k_ref.shape[0] // chunk):
            part = slice(i * chunk, (i + 1) * chunk)
            key = k_ref[part, :]
            value = v_ref[part, :]
            key_t = key.astype(f32).T.astype(bf16)
            g_key, g_value = [], []
            for e in range(2):
                probs = jnp.exp(matmul(key, queries[e]) - sums[e])
                g_scores = (probs * (matmul(value, grads[e]) - inners[e])).astype(bf16)
                g_key.append(matmul(g_scores, query))
                g_value.append(matmul(probs.astype(bf16), grad))
                g_query[e] = g_query[e] + matmul(key_t[e * size : (e + 1) * size], g_scores)
            gk_ref[part, :] = jnp.where(first, g_key[0], g_key[1]).astype(gk_ref.dtype)
            gv_ref[part, :] = jnp.where(first, g_value[0], g_value[1]).astype(gv_ref.dtype)
    gq_ref[...] = jnp.concatenate(g_query, axis=0).T.astype(gq_ref.dtype)


def attend_back(query, key, key_peer, value, value_peer, grad, attended, lse):
    rows, width = query.shape
    size = width // HEADS
    spec = pl.BlockSpec((rows, 2 * size), lambda h: (0, h))
    low, full = shaped((rows, width), bf16), shaped((rows, width), f32)
    return pl.pallas_call(
        functools.partial(attend_back_kernel, size=size, chunk=rows),
        grid=(HEADS // 2,),
        in_specs=[spec] * 8,
        out_specs=[spec] * 5,
        out_shape=[low, full, low, full, low],
        compiler_params=params("arbitrary"),
        cost_estimate=cost(),
        name="attend_back",
    )(query, key, key_peer, value, value_peer, grad, attended, lse)


def whole(shape):
    return pl.BlockSpec(shape, lambda i, s: (0,) * len(shape))


def gather_rows_kernel(at_ref, own_ref, peer_ref, out_ref, rows_ref):
    core = at_ref[0]
    strips, part = own_ref.shape[:2]
    half = out_ref.shape[0]
    for j in range(strips):
        start, count = at_ref[1 + j], at_ref[1 + strips + j]
        for ref, which in ((own_ref, core), (peer_ref, 1 - core)):
            for i in range(part):
                local = which * part + i
                row = start + local - core * half
                here = jnp.logical_and(local < count, jnp.logical_and(row >= 0, row < half))
                rows_ref[jnp.where(here, row, half)] = ref[j, i]
    out_ref[...] = rows_ref[:half]


def gather_rows(at, own, peer, half):
    strips, part, grid, width = own.shape
    out = (half, grid, width)
    return pl.pallas_call(
        gather_rows_kernel,
        grid_spec=pltpu.PrefetchScalarGridSpec(
            num_scalar_prefetch=1,
            grid=(1,),
            in_specs=[whole(own.shape)] * 2,
            out_specs=whole(out),
            scratch_shapes=[pltpu.VMEM((half + 1, grid, width), bf16)],
        ),
        out_shape=shaped(out, bf16),
        compiler_params=params("arbitrary"),
        cost_estimate=cost(),
        name="gather_rows",
    )(at, own, peer)


def spread_rows_kernel(at_ref, own_ref, peer_ref, out_ref, rows_ref):
    core = at_ref[0]
    strips, part = out_ref.shape[:2]
    half = own_ref.shape[0]
    rows_ref[pl.ds(core * half, half)] = own_ref[...]
    rows_ref[pl.ds((1 - core) * half, half)] = peer_ref[...]
    rows_ref[2 * half] = jnp.zeros(rows_ref.shape[1:], bf16)
    for j in range(strips):
        start, count = at_ref[1 + j], at_ref[1 + strips + j]
        for i in range(part):
            local = core * part + i
            out_ref[j, i] = rows_ref[jnp.where(local < count, start + local, 2 * half)]


def spread_rows(at, own, peer, strips, capacity):
    half, grid, width = own.shape
    out = (strips, capacity // 2, grid, width)
    return pl.pallas_call(
        spread_rows_kernel,
        grid_spec=pltpu.PrefetchScalarGridSpec(
            num_scalar_prefetch=1,
            grid=(1,),
            in_specs=[whole(own.shape)] * 2,
            out_specs=whole(out),
            scratch_shapes=[pltpu.VMEM((2 * half + 1, grid, width), bf16)],
        ),
        out_shape=shaped(out, bf16),
        compiler_params=params("arbitrary"),
        cost_estimate=cost(),
        name="spread_rows",
    )(at, own, peer)


def normalise(values):
    centred = values - jnp.mean(values, axis=-1, keepdims=True)
    scale = lax.rsqrt(jnp.mean(centred * centred, axis=-1, keepdims=True) + 1e-06)
    return centred * scale, scale


def norm_back(grad, normed, scale):
    return scale * (
        grad
        - jnp.mean(grad, axis=-1, keepdims=True)
        - normed * jnp.mean(grad * normed, axis=-1, keepdims=True)
    )


def column_sum(values):
    return jnp.sum(values, axis=0, keepdims=True)


PATCH, GAIN1, SHIFT1, QUERY, VALUE, OUT, GAIN2, SHIFT2, DOWN = range(9)
VECTORS = 9
UP_AT = 9
POS_AT = 16
TABLE = 96
POS_ROWS = 64


def patch_kernel(base_ref, left_ref, right_ref, out_ref):
    half = left_ref.shape[1]
    out_ref[:, :half] = matmul(base_ref[...], left_ref[...]).astype(bf16)
    out_ref[:, half:] = matmul(base_ref[...], right_ref[...]).astype(bf16)


def embed_patches(base, left, right):
    group, rows, length = base.shape
    half = left.shape[1]
    return pl.pallas_call(
        patch_kernel,
        grid=(group,),
        in_specs=[
            pl.BlockSpec((None, rows, length), lambda t: (t, 0, 0)),
            pl.BlockSpec((length, half), lambda t: (0, 0)),
            pl.BlockSpec((length, half), lambda t: (0, 0)),
        ],
        out_specs=pl.BlockSpec((None, rows, 2 * half), lambda t: (t, 0, 0)),
        out_shape=shaped((group, rows, 2 * half), bf16),
        compiler_params=params("arbitrary"),
        cost_estimate=cost(),
        name="embed_patches",
    )(base, left, right)


def enter_kernel(
    at_ref, patches_ref, spread_ref, table_ref, ql_ref, qr_ref, kl_ref, kr_ref, vl_ref, vr_ref,
    embed_ref, in_ref, q_ref, k_ref, v_ref,
):
    def vector(row):
        return table_ref[row : row + 1, :]

    place_rows = jnp.dot(
        spread_ref[...],
        table_ref[POS_AT : POS_AT + POS_ROWS, :],
        precision=HIGH_ACCURACY,
        preferred_element_type=f32,
    )
    embed = patches_ref[...].astype(f32) + vector(PATCH) + place_rows
    embed_ref[...] = embed
    normed, _ = normalise(embed)
    attn_in = (normed * vector(GAIN1) + vector(SHIFT1)).astype(bf16)
    in_ref[...] = attn_in
    half = ql_ref.shape[1]
    for ref, weights, bias, scale in (
        (q_ref, (ql_ref, qr_ref), vector(QUERY), 0.125),
        (k_ref, (kl_ref, kr_ref), None, None),
        (v_ref, (vl_ref, vr_ref), vector(VALUE), None),
    ):
        for columns, weight in zip((slice(0, half), slice(half, 2 * half)), weights):
            rows = matmul(attn_in, weight[...])
            if bias is not None:
                rows = rows + bias[:, columns]
            if scale is not None:
                rows = rows * scale
            ref[:, columns] = rows.astype(bf16)


def enter(at, patches, spread, table, weights, blocks=2):
    rows, width = patches.shape
    block = rows // blocks
    part = pl.BlockSpec((block, width), lambda t, a: (t, 0))
    weight = pl.BlockSpec(weights[0].shape, lambda t, a: (0, 0))
    low = shaped((rows, width), bf16)
    return pl.pallas_call(
        enter_kernel,
        grid_spec=pltpu.PrefetchScalarGridSpec(
            num_scalar_prefetch=1,
            grid=(blocks,),
            in_specs=[
                part,
                pl.BlockSpec((None, block, POS_ROWS), lambda t, a: (a[0], t, 0)),
                pl.BlockSpec(table.shape, lambda t, a: (0, 0)),
                *([weight] * 6),
            ],
            out_specs=[part] * 5,
        ),
        out_shape=[shaped((rows, width), f32), low, low, low, low],
        compiler_params=params("arbitrary"),
        cost_estimate=cost(),
        name="enter",
    )(at, patches, spread, table, *weights)


def mlp_kernel(
    attended_ref, embed_ref, table_ref, ol_ref, or_ref, up_ref, bias_ref, down_ref,
    resid_ref, in_ref, hidden_ref, slope_ref, out_ref, total,
):
    step = pl.program_id(0)

    def vector(row):
        return table_ref[row : row + 1, :]

    @pl.when(step == 0)
    def _():
        half = ol_ref.shape[1]
        for columns, weight in ((slice(0, half), ol_ref), (slice(half, 2 * half), or_ref)):
            resid_ref[:, columns] = (
                embed_ref[:, columns]
                + matmul(attended_ref[...], weight[...])
                + vector(OUT)[:, columns]
            )
        resid = resid_ref[...]
        normed, _ = normalise(resid)
        in_ref[...] = (normed * vector(GAIN2) + vector(SHIFT2)).astype(bf16)
        total[...] = resid + vector(DOWN)

    upper = matmul(in_ref[...], up_ref[...]) + bias_ref[...]
    below = 0.5 + 0.5 * lax.erf(upper * 0.7071067811865476)
    hidden = (upper * below).astype(bf16)
    hidden_ref[...] = hidden
    slope_ref[...] = (below + upper * (0.3989422804014327 * jnp.exp(-0.5 * upper * upper))).astype(
        slope_ref.dtype
    )
    total[...] += matmul(hidden, down_ref[...])

    @pl.when(step == pl.num_programs(0) - 1)
    def _():
        out_ref[...] = total[...].astype(bf16)


def mlp(attended, embed, table, w_out, w_up, b_up, w_down):
    rows, width = embed.shape
    blocks = w_up.shape[0]
    ff = blocks * width
    fixed = pl.BlockSpec((rows, width), lambda t: (0, 0))
    columns = pl.BlockSpec((rows, width), lambda t: (0, t))
    return pl.pallas_call(
        mlp_kernel,
        grid=(blocks,),
        in_specs=[
            fixed,
            fixed,
            pl.BlockSpec(table.shape, lambda t: (0, 0)),
            *([pl.BlockSpec(w_out[0].shape, lambda t: (0, 0))] * 2),
            pl.BlockSpec((None, width, width), lambda t: (t, 0, 0)),
            pl.BlockSpec((1, width), lambda t: (0, t)),
            pl.BlockSpec((width, width), lambda t: (t, 0)),
        ],
        out_specs=[fixed, fixed, columns, columns, fixed],
        out_shape=[
            shaped((rows, width), f32),
            shaped((rows, width), bf16),
            shaped((rows, ff), bf16),
            shaped((rows, ff), f32),
            shaped((rows, width), bf16),
        ],
        scratch_shapes=[pltpu.VMEM((rows, width), f32)],
        compiler_params=params("arbitrary"),
        cost_estimate=cost(),
        name="mlp",
    )(attended, embed, table, *w_out, w_up, b_up, w_down)


def mlp_back_kernel(
    g_ref, slope_ref, resid_ref, table_ref, ol_ref, or_ref, up_ref, down_ref,
    upper_ref, resid_grad_ref, low_ref, att_ref, sums_ref, total,
):
    step = pl.program_id(0)

    @pl.when(step == 0)
    def _():
        total[...] = jnp.zeros_like(total)
        sums_ref[...] = jnp.zeros_like(sums_ref)

    g_upper = slope_ref[...].astype(f32) * right_trans(g_ref[...], down_ref[...])
    sums_ref[pl.ds(8 + step, 1), :] = column_sum(g_upper)
    g_upper_low = g_upper.astype(bf16)
    upper_ref[...] = g_upper_low
    total[...] += right_trans(g_upper_low, up_ref[...])

    @pl.when(step == pl.num_programs(0) - 1)
    def _():
        grad = total[...]
        g_out = g_ref[...].astype(f32)
        normed, scale = normalise(resid_ref[...])
        g_resid = g_out + norm_back(grad * table_ref[GAIN2 : GAIN2 + 1, :], normed, scale)
        resid_grad_ref[...] = g_resid
        g_resid_low = g_resid.astype(bf16)
        low_ref[...] = g_resid_low
        half = ol_ref.shape[1]
        att_ref[...] = (
            right_trans(g_resid_low[:, :half], ol_ref[...])
            + right_trans(g_resid_low[:, half:], or_ref[...])
        ).astype(bf16)
        sums_ref[0:1, :] = column_sum(g_resid)
        sums_ref[1:2, :] = column_sum(grad * normed)
        sums_ref[2:3, :] = column_sum(grad)
        sums_ref[3:4, :] = column_sum(g_out)


def mlp_back(g_out, slope, resid, table, w_out, w_up, w_down):
    rows, width = g_out.shape
    blocks = w_up.shape[0]
    ff = blocks * width
    fixed = pl.BlockSpec((rows, width), lambda t: (0, 0))
    columns = pl.BlockSpec((rows, width), lambda t: (0, t))
    sums = (8 + 8 * (-(-blocks // 8)), width)
    return pl.pallas_call(
        mlp_back_kernel,
        grid=(blocks,),
        in_specs=[
            fixed,
            columns,
            fixed,
            pl.BlockSpec(table.shape, lambda t: (0, 0)),
            *([pl.BlockSpec(w_out[0].shape, lambda t: (0, 0))] * 2),
            pl.BlockSpec((None, width, width), lambda t: (t, 0, 0)),
            pl.BlockSpec((width, width), lambda t: (t, 0)),
        ],
        out_specs=[columns, fixed, fixed, fixed, pl.BlockSpec(sums, lambda t: (0, 0))],
        out_shape=[
            shaped((rows, ff), bf16),
            shaped((rows, width), f32),
            shaped((rows, width), bf16),
            shaped((rows, width), bf16),
            shaped(sums, f32),
        ],
        scratch_shapes=[pltpu.VMEM((rows, width), f32)],
        compiler_params=params("arbitrary"),
        cost_estimate=cost(),
        name="mlp_back",
    )(g_out, slope, resid, table, *w_out, w_up, w_down)


def leave_kernel(
    at_ref, gq_ref, gk_ref, gkp_ref, gv_ref, gvp_ref, embed_ref, resid_ref, spread_ref, table_ref,
    ql_ref, qr_ref, kl_ref, kr_ref, vl_ref, vr_ref, q_ref, k_ref, v_ref, out_ref, sums_ref, pos_ref,
):
    @pl.when(pl.program_id(0) == 0)
    def _():
        sums_ref[...] = jnp.zeros_like(sums_ref)
        pos_ref[...] = jnp.zeros_like(pos_ref)

    g_query = gq_ref[...].astype(f32) * 0.125
    g_query_low = g_query.astype(bf16)
    g_key_low = (gk_ref[...] + gkp_ref[...].astype(f32)).astype(bf16)
    g_value_low = (gv_ref[...] + gvp_ref[...].astype(f32)).astype(bf16)
    q_ref[...] = g_query_low
    k_ref[...] = g_key_low
    v_ref[...] = g_value_low
    half = ql_ref.shape[1]
    grad = jnp.zeros(embed_ref.shape, f32)
    for low, weights in (
        (g_query_low, (ql_ref, qr_ref)),
        (g_key_low, (kl_ref, kr_ref)),
        (g_value_low, (vl_ref, vr_ref)),
    ):
        grad = grad + right_trans(low[:, :half], weights[0][...])
        grad = grad + right_trans(low[:, half:], weights[1][...])
    normed, scale = normalise(embed_ref[...])
    g_embed = resid_ref[...] + norm_back(grad * table_ref[GAIN1 : GAIN1 + 1, :], normed, scale)
    out_ref[...] = g_embed.astype(bf16)
    sums_ref[0:1, :] += column_sum(g_embed)
    sums_ref[1:2, :] += column_sum(grad * normed)
    sums_ref[2:3, :] += column_sum(grad)
    sums_ref[3:4, :] += column_sum(g_query)
    sums_ref[4:5, :] += column_sum(g_value_low.astype(f32))
    pos_ref[...] += jnp.dot(
        spread_ref[...], g_embed, precision=HIGH_ACCURACY, preferred_element_type=f32
    )


def leave(
    at, g_query, g_key, g_key_peer, g_value, g_value_peer, embed, g_resid, spread, table,
    weights, blocks=2,
):
    rows, width = embed.shape
    block = rows // blocks
    part = pl.BlockSpec((block, width), lambda t, a: (t, 0))
    weight = pl.BlockSpec(weights[0].shape, lambda t, a: (0, 0))
    low = shaped((rows, width), bf16)
    return pl.pallas_call(
        leave_kernel,
        grid_spec=pltpu.PrefetchScalarGridSpec(
            num_scalar_prefetch=1,
            grid=(blocks,),
            in_specs=[part] * 7
            + [
                pl.BlockSpec((None, POS_ROWS, block), lambda t, a: (a[0], 0, t)),
                pl.BlockSpec(table.shape, lambda t, a: (0, 0)),
                *([weight] * 6),
            ],
            out_specs=[part] * 4
            + [
                pl.BlockSpec((8, width), lambda t, a: (0, 0)),
                pl.BlockSpec((POS_ROWS, width), lambda t, a: (0, 0)),
            ],
        ),
        out_shape=[low] * 4 + [shaped((8, width), f32), shaped((POS_ROWS, width), f32)],
        compiler_params=params("arbitrary"),
        cost_estimate=cost(),
        name="leave",
    )(
        at, g_query, g_key, g_key_peer, g_value, g_value_peer, embed, g_resid, spread, table,
        *weights,
    )


def weight_grad_kernel(at_ref, left_ref, right_ref, send_ref, keep_ref, total):
    core = at_ref[0]
    group, rows, _ = send_ref.shape
    total[...] = left_trans(left_ref[...], right_ref[...])
    for h in range(group):
        sent = pl.multiple_of((2 * h + 1 - core) * rows, 8)
        kept = pl.multiple_of((2 * h + core) * rows, 8)
        send_ref[h] = total[pl.ds(sent, rows), :].astype(bf16)
        keep_ref[h] = total[pl.ds(kept, rows), :]


def weight_grad(at, left, right, his, light=False):
    tokens, m = left.shape
    n = right.shape[1]
    rows = m // (2 * his)
    tall = min(m, 768)
    h = tall // (2 * rows)
    wide = 768
    blocks = n // wide
    out = pl.BlockSpec((h, None, rows, wide), lambda i, j, a: (i, j, 0, 0))
    shape = (his, blocks, rows, wide)
    return pl.pallas_call(
        weight_grad_kernel,
        grid_spec=pltpu.PrefetchScalarGridSpec(
            num_scalar_prefetch=1,
            grid=(m // tall, blocks),
            in_specs=[
                pl.BlockSpec((tokens, tall), lambda i, j, a: (0, i)),
                pl.BlockSpec((tokens, wide), lambda i, j, a: (0, j)),
            ],
            out_specs=[out, out],
            scratch_shapes=[pltpu.VMEM((tall, wide), f32)],
        ),
        out_shape=[shaped(shape, bf16), shaped(shape, f32)],
        compiler_params=params("arbitrary", "arbitrary"),
        cost_estimate=cost(light),
        name="weight_grad",
    )(at, left, right)


def proj_grad_kernel(
    at_ref, in_ref, att_ref, gq_ref, gk_ref, gv_ref, go_ref, send_ref, keep_ref, total
):
    core = at_ref[0]
    his, _, rows, _ = send_ref.shape
    pairs = ((in_ref, gq_ref), (in_ref, gk_ref), (in_ref, gv_ref), (att_ref, go_ref))
    for i, (left, right) in enumerate(pairs):
        total[...] = left_trans(left[...], right[...])
        for h in range(his):
            sent = pl.multiple_of((2 * h + 1 - core) * rows, 8)
            kept = pl.multiple_of((2 * h + core) * rows, 8)
            send_ref[h, i] = total[pl.ds(sent, rows), :].astype(bf16)
            keep_ref[h, i] = total[pl.ds(kept, rows), :]


def proj_grad(at, attn_in, attended, g_query, g_key, g_value, g_resid, his):
    tokens, width = attn_in.shape
    rows = width // (2 * his)
    out = (his, 4, rows, width)
    return pl.pallas_call(
        proj_grad_kernel,
        grid_spec=pltpu.PrefetchScalarGridSpec(
            num_scalar_prefetch=1,
            grid=(1,),
            in_specs=[whole(attn_in.shape)] * 6,
            out_specs=[whole(out)] * 2,
            scratch_shapes=[pltpu.VMEM((width, width), f32)],
        ),
        out_shape=[shaped(out, bf16), shaped(out, f32)],
        compiler_params=params("arbitrary"),
        cost_estimate=cost(),
        name="proj_grad",
    )(at, attn_in, attended, g_query, g_key, g_value, g_resid)


class Place:
    def __init__(self, group):
        self.group = group
        self.images = lax.axis_size("img")
        self.strips = lax.axis_size("strip")
        assert group == 2 and self.strips == 4
        self.img = lax.axis_index("img")
        self.core = self.img % 2
        self.z = lax.axis_index("strip")
        self.bits = [1 << k for k in range(1, self.images.bit_length() - 1)]
        assert self.images == 2 << len(self.bits)

    def flat(self, img, z):
        return img * self.strips + z

    def swap_core(self, values):
        return lax.ppermute(values, "img", [(i, i ^ 1) for i in range(self.images)])

    def across_img(self, values, bit):
        return lax.ppermute(values, "img", [(i, i ^ bit) for i in range(self.images)])

    def along_z(self, values, r):
        return lax.ppermute(values, "strip", [(z, z ^ r) for z in range(self.strips)])


def pick(values, index, axis=0):
    return lax.dynamic_index_in_dim(values, index, axis, keepdims=False)


def after(values, *others):
    return lax.optimization_barrier((values,) + others)[0]


def collect(values, *others):
    values = tuple(values)
    return lax.optimization_barrier(values + others)[: len(values)]


def exchange(values):
    return lax.all_to_all(values, "strip", 0, 0, tiled=True)


class Gather:
    def __init__(self, place, held, bits=()):
        self.place = place
        self.held = held
        self.bits = list(bits)

    def halves(self):
        middle = self.held.shape[-1] // 2
        return [
            Gather(self.place, self.held[..., columns], self.bits)
            for columns in (slice(0, middle), slice(middle, None))
        ]

    def along_z(self, *others):
        if others:
            self.held = after(self.held, *others)
        self.held = exchange(jnp.broadcast_to(self.held, (self.place.strips,) + self.held.shape))

    def z_done(self, *others):
        (self.held,) = collect([self.held], *others)

    def over(self, bit, *others):
        if others:
            self.held = after(self.held, *others)
        self.bit = bit
        self.got = self.place.across_img(self.held, bit)

    def done(self, *others):
        (got,) = collect([self.got], *others)
        self.bits = sorted(self.bits + [self.bit], reverse=True)
        axis = self.bits.index(self.bit)
        self.held = join(self.held, got, axis, (self.place.img // self.bit) % 2)

    def last(self, *others):
        if others:
            self.held = after(self.held, *others)
        self.other = self.place.swap_core(self.held)

    def last_done(self, *others):
        (self.other,) = collect([self.other], *others)

    def rows(self, start=0, stop=None):
        axis = len(self.bits)
        full = join(self.held[..., start:stop, :], self.other[..., start:stop, :], axis, self.place.core)
        return full.reshape((-1,) + full.shape[-2:])


def join(mine, other, axis, at):
    spot = [1] * (mine.ndim + 1)
    spot[axis] = 2
    where = jnp.arange(2, dtype=jnp.int32).reshape(spot) == at
    return jnp.where(where, jnp.expand_dims(mine, axis), jnp.expand_dims(other, axis))


class Scatter:
    def __init__(self, place, send, keep):
        self.place = place
        self.bits = place.bits[::-1]
        self.send = send
        self.keep = keep

    def first(self):
        self.got = self.place.swap_core(self.send)

    def first_done(self, *others):
        (got,) = collect([self.got], *others)
        shape = (2,) * len(self.bits) + self.send.shape[1:]
        self.part = self.keep.reshape(shape) + got.reshape(shape).astype(f32)

    def halves(self, axis=None):
        axis = len(self.bits) if axis is None else axis % self.part.ndim
        parts = []
        middle = self.part.shape[axis] // 2
        for start, stop in ((0, middle), (middle, self.part.shape[axis])):
            one = Scatter(self.place, None, None)
            one.part = lax.slice_in_dim(self.part, start, stop, axis=axis)
            parts.append(one)
        return parts

    def over(self, bit):
        self.bit = bit
        axis = self.bits.index(bit)
        self.sent = pick(self.part, 1 - (self.place.img // bit) % 2, axis).astype(bf16)
        self.got = self.place.across_img(self.sent, bit)

    def done(self, *others):
        (got,) = collect([self.got], *others)
        axis = self.bits.index(self.bit)
        self.part = pick(self.part, (self.place.img // self.bit) % 2, axis) + got.astype(f32)
        self.bits = [b for b in self.bits if b != self.bit]

    def by_strip(self):
        blocks, rows, columns = self.part.shape
        part = self.part.reshape(blocks, self.place.strips, -1, columns)
        return part.transpose(1, 0, 2, 3).reshape(self.place.strips, -1, columns)


class Last:
    def __init__(self, values):
        self.sent = values.astype(bf16)
        self.got = exchange(self.sent)

    def done(self, *others):
        (got,) = collect([self.got], *others)
        return jnp.sum(got.astype(f32), axis=0)


def split_rows(place, values):
    images, rows = values.shape[:2]
    values = values.reshape((images, 2, rows // 2) + values.shape[2:])
    return pick(values, place.core, 1), pick(values, 1 - place.core, 1)


def pair_up(place, mine, other):
    return jnp.where(
        place.core == 0, jnp.concatenate([mine, other]), jnp.concatenate([other, mine])
    )


def from_chip(place, moved, shape):
    images, rows = shape[0], shape[1] // 2
    moved = moved.reshape((2, images) + moved.shape[1:])
    mine, sent = pick(moved, place.core), pick(moved, 1 - place.core)
    got = place.swap_core(sent)
    low = jnp.where(place.core == 0, mine, got)
    high = jnp.where(place.core == 0, got, mine)
    return jnp.concatenate([low, high], axis=1)


def body(
    pixels,
    cotangent,
    resize,
    patch_index,
    slot_image,
    strip_rows,
    patch_weight,
    pos_grid,
    patch_bias,
    attention_norm_gain,
    attn_shift,
    query_weight,
    query_bias,
    key_weight,
    value_weight,
    value_bias,
    out_weight,
    out_bias,
    mlp_gain,
    mlp_shift,
    up_weight,
    up_bias,
    down_weight,
    down_bias,
):
    group, capacity, grid, pixel_len = pixels.shape
    width = cotangent.shape[3]
    ff = up_weight.shape[1]
    local_rows = capacity * grid
    tokens = group * local_rows
    place = Place(group)
    devices = place.images * place.strips
    his = place.images // 2
    first_slot = place.img * group
    shard = patch_bias.shape[0]
    ups = up_bias.shape[0]
    columns = width // 2
    bits = place.bits

    vectors = (
        patch_bias,
        attention_norm_gain,
        attn_shift,
        query_bias,
        value_bias,
        out_bias,
        mlp_gain,
        mlp_shift,
        down_bias,
    )
    pieces = ups // shard
    small = jnp.concatenate(
        [
            jnp.stack(vectors + tuple(up_bias[i * shard : (i + 1) * shard] for i in range(pieces))),
            jnp.zeros((POS_AT - VECTORS - pieces, shard), bf16),
            pos_grid,
            jnp.zeros((TABLE - POS_AT - BASE * BASE, shard), bf16),
        ]
    )
    lane = width // (TABLE // 16)
    small = jnp.pad(small, ((0, 0), (0, lane - shard))).reshape(-1, 16, lane)
    small = jnp.concatenate(list(small), axis=1)
    proj = jnp.concatenate([query_weight, key_weight, value_weight, out_weight, small])

    size_count = resize.shape[0]
    slot_ids = lax.dynamic_slice_in_dim(slot_image, first_slot, group)
    picked = slot_ids[:, None] == jnp.arange(patch_index.shape[0], dtype=jnp.int32)[None, :]
    size_index = jnp.sum(jnp.where(picked, patch_index[None, :], 0), axis=1)
    sizes = jnp.append(size_index, size_count).astype(jnp.int32)
    half = grid // 2
    image_counts = pick(strip_rows, (place.img // 2) * 2 * group + place.z)
    starts = jnp.cumsum(image_counts) - image_counts
    at = jnp.concatenate([place.core[None], starts, image_counts]).astype(jnp.int32)

    spread = bilinear(grid, BASE)
    spread = (spread[:, None, :, None] * spread[None, :, None, :]).reshape(2, half * grid, -1)
    spread = np.pad(spread, ((0, 0), (0, 0), (0, POS_ROWS - BASE * BASE)))
    spread_t = jnp.asarray(np.ascontiguousarray(spread.transpose(0, 2, 1)))
    spread = jnp.asarray(spread)

    whole_patch, packed = Gather(place, patch_weight), Gather(place, proj)
    blocks = ff // width
    both = Gather(
        place,
        jnp.concatenate(
            [down_weight]
            + [up_weight[:, i * width : (i + 1) * width] for i in range(blocks)]
        ),
    )
    whole_patch.along_z()
    base_pixels = mix(sizes, resize, pixels.reshape(group, local_rows, pixel_len))
    whole_patch.z_done(base_pixels)
    left, right = whole_patch.halves()
    for k in range(len(bits)):
        if k == len(bits) - 1:
            packed.along_z(left.held, right.held)
        left.over(bits[k])
        right.over(bits[-1 - k])
        left.done()
        right.done()
    packed.z_done()
    left.last(packed.held, right.held)
    right.last(packed.held, left.held)
    left.last_done()
    right.last_done()
    w_left, w_right = left.rows().reshape(-1, columns), right.rows().reshape(-1, columns)
    packs = packed.halves()
    packs[0].over(bits[0], left.other)
    packs[1].over(bits[-1], left.other)
    both.along_z(left.other, right.other)
    patches = embed_patches(base_pixels, w_left, w_right).reshape(group, capacity, grid, width)
    packs[0].done()
    packs[1].done()
    for k in range(1, len(bits)):
        packs[0].over(bits[k])
        packs[1].over(bits[-1 - k])
        packs[0].done(patches)
        packs[1].done(patches)
    both.z_done(patches)
    downs_w = Gather(place, both.held[:, : down_weight.shape[0]], both.bits)
    ups_w = Gather(place, both.held[:, down_weight.shape[0] :], both.bits)
    patch_mine, patch_sent = split_rows(place, patches)
    patch_got = place.swap_core(after(patch_sent, packs[0].held, packs[1].held))
    patch_moved = exchange(pair_up(place, patch_mine, patch_got))
    packs[0].last(patch_got)
    packs[1].last(patch_got)
    ups_w.over(bits[-1], patch_got)
    downs_w.over(bits[0], patch_got)
    for k in range(1, len(bits) - 1):
        ups_w.done()
        downs_w.done()
        ups_w.over(bits[-1 - k])
        downs_w.over(bits[k])
    cot_mine, cot_sent = split_rows(place, cotangent)
    cot_got = place.swap_core(after(cot_sent, patch_got))
    cot_pair = pair_up(place, cot_mine, cot_got)

    halves = [
        [p.rows(i * shard, (i + 1) * shard).reshape(width, columns) for p in packs]
        for i in range(4)
    ]
    in_weights = [*halves[0], *halves[1], *halves[2]]
    w_out = halves[3]
    flat = jnp.concatenate([p.rows(4 * shard) for p in packs], axis=-1)
    table = (
        flat.reshape(devices, 16, TABLE // 16, lane)[..., :shard]
        .transpose(2, 1, 0, 3)
        .reshape(TABLE, width)
        .astype(f32)
    )
    b_up = (
        table[UP_AT : UP_AT + pieces]
        .reshape(pieces, devices, shard)
        .transpose(1, 0, 2)
        .reshape(1, ff)
    )
    (patch_moved,) = collect([patch_moved], table, b_up, cot_pair, *in_weights, *w_out)
    ups_w.done(patch_moved)
    downs_w.done(patch_moved)
    patch_peer = place.swap_core(patch_moved)
    patches = gather_rows(at, patch_moved, patch_peer, half).reshape(-1, width)
    if len(bits) > 1:
        ups_w.over(bits[0], patch_moved)
        downs_w.over(bits[-1], patch_moved)
    cot_moved = exchange(after(cot_pair, patch_moved))

    embed, attn_in, query, key, value = enter(at, patches, spread, table, in_weights)
    if len(bits) > 1:
        ups_w.done(query)
        downs_w.done(query)
    (cot_moved,) = collect([cot_moved], query)
    key_peer = place.swap_core(after(key, ups_w.held, downs_w.held, cot_moved))
    value_peer = place.swap_core(after(value, ups_w.held, downs_w.held, cot_moved))
    ups_w.last(key_peer, value_peer)
    downs_w.last(key_peer, value_peer)
    cot_peer = place.swap_core(after(cot_moved, key_peer, value_peer))
    attended, lse = attend(query, key, key_peer, value, value_peer)
    ups_w.last_done(attended)
    downs_w.last_done(attended)
    (cot_peer,) = collect([cot_peer], attended)
    w_up = (
        ups_w.rows()
        .reshape(devices, blocks, shard, width)
        .transpose(1, 0, 2, 3)
        .reshape(blocks, width, width)
    )
    w_down = downs_w.rows().reshape(ff, width)
    resid, mlp_in, hidden, slope, final = mlp(attended, embed, table, w_out, w_up, b_up, w_down)
    final_peer = place.swap_core(final)
    g_out = gather_rows(after(at, final), cot_moved, cot_peer, half).reshape(-1, width)

    early, late = bits[: len(bits) // 2], bits[len(bits) // 2 :][::-1]
    down = Scatter(place, *weight_grad(at, hidden, g_out, his))
    (final_peer,) = collect([final_peer], down.send)
    down.send = after(down.send, final_peer)
    down.first()
    image = (half, grid, width)
    final_pieces = spread_rows(
        at, final.reshape(image), final_peer.reshape(image), place.strips, capacity
    )
    down.first_done(final_pieces)
    for bit in late[:-1]:
        down.over(bit)
        down.done()
    down.over(late[-1])
    final_moved = exchange(after(final_pieces, down.sent))
    g_upper, g_resid, g_resid_low, g_att, sums_two = mlp_back(
        after(g_out, final_pieces, down.sent), slope, resid, table, w_out, w_up, w_down
    )
    up = Scatter(place, *weight_grad(at, mlp_in, g_upper, his, True))
    down.done(up.send)
    (final_moved,) = collect([final_moved], up.send)
    up.send = after(up.send, final_moved, down.part)
    up.first()
    up.first_done()
    for bit in late[:-1]:
        up.over(bit)
        up.done()
    up.over(late[-1])
    for bit in early[:-1]:
        down.over(bit)
        down.done()
    if early:
        down.over(early[-1])
    g_query, g_key, g_key_peer, g_value, g_value_peer = attend_back(
        query, key, key_peer, value, value_peer, after(g_att, up.sent, down.sent), attended, lse
    )
    up.done(g_query)
    if early:
        down.done(g_query)
    g_key_got = place.swap_core(after(g_key_peer, up.part, down.part))
    g_value_got = place.swap_core(g_value_peer)
    for bit in early[:-1]:
        up.over(bit)
        up.done()
    if early:
        up.over(early[-1])
    g_query, g_key, g_value, g_embed, sums_one, g_pos = leave(
        at,
        after(g_query, up.sent),
        g_key,
        g_key_got,
        g_value,
        g_value_got,
        embed,
        g_resid,
        spread_t,
        table,
        in_weights,
    )
    if early:
        up.done(g_embed)
    g_embed_peer = place.swap_core(g_embed)
    pieces_back = spread_rows(
        at, g_embed.reshape(image), g_embed_peer.reshape(image), place.strips, capacity
    )
    back = exchange(pieces_back)
    small = after(jnp.concatenate([sums_one, sums_two, g_pos]), pieces_back)
    small_got = place.swap_core(small)
    block_out = from_chip(place, after(final_moved, pieces_back), cotangent.shape)
    proj = Scatter(
        place,
        *proj_grad(
            after(at, pieces_back), attn_in, attended, g_query, g_key, g_value, g_resid_low, his
        ),
    )
    back, small_got = collect([back, small_got], proj.send, block_out)
    small = small + small_got
    sent = jnp.concatenate([down.by_strip(), up.by_strip()], axis=1)
    last = Last(after(sent, back))
    proj.send = after(proj.send, back)
    proj.first()
    g_patches = from_chip(place, back, cotangent.shape).reshape(tokens, width)
    small_got = place.along_z(after(small, back), 1)
    patch = Scatter(
        place,
        *weight_grad(
            at,
            base_pixels.reshape(tokens, pixel_len),
            after(g_patches, last.sent),
            his,
        ),
    )
    small = small + collect([small_got], patch.send)[0]
    proj.first_done(patch.send)
    projs = proj.halves()
    patch.first()
    projs[0].over(bits[-1])
    projs[1].over(bits[0])
    patch.first_done()
    patches = patch.halves(-1)
    patches[0].over(bits[-1])
    patches[1].over(bits[0])
    small_got = place.along_z(after(small, patch.part), 2)
    pixel_grad = unmix(
        sizes,
        resize,
        w_left,
        w_right,
        after(
            g_patches, small, patches[0].sent, patches[1].sent, projs[0].sent, projs[1].sent
        ).reshape(group, local_rows, width),
    )
    for scatter in (*patches, *projs):
        scatter.done(pixel_grad)
    small = small + collect([small_got], pixel_grad)[0]
    sums = last.done(pixel_grad)
    patches[0].part = after(patches[0].part, small)
    patches[1].part = after(patches[1].part, small)
    for k in range(1, len(bits)):
        small_got = place.across_img(small, bits[k])
        patches[0].over(bits[-1 - k])
        patches[1].over(bits[k])
        projs[0].over(bits[-1 - k])
        projs[1].over(bits[k])
        small = small + small_got
        for scatter in (*patches, *projs):
            scatter.done()
    small_last = place.across_img(small, bits[0])
    patches[0].part = after(patches[0].part, small)
    tail = Last(
        jnp.concatenate(
            [
                jnp.concatenate([p.by_strip() for p in patches], axis=-1),
                *(p.by_strip() for p in projs),
            ],
            axis=1,
        )
    )
    small = small + small_last
    tail = tail.done(small)
    pixel_grad = pixel_grad.reshape(pixels.shape)

    flat_index = place.flat(place.img, place.z)
    own = lax.dynamic_slice_in_dim(small, flat_index * shard, shard, axis=1)
    ahead = sums_one.shape[0]
    behind = ahead + sums_two.shape[0]
    up_sums = small[ahead + 8 : ahead + 8 + ff // width].reshape(-1)
    s_up_bias = lax.dynamic_slice_in_dim(up_sums, flat_index * ups, ups)
    down_rows = down_weight.shape[0]
    s_down = sums[:down_rows]
    s_up = sums[down_rows:].reshape(ff // width, shard, width).transpose(1, 0, 2).reshape(shard, ff)
    patch_rows = patch_weight.shape[0]
    s_patch = tail[:patch_rows]
    s_proj = tail[patch_rows:].reshape(4, shard, width)

    return (
        block_out,
        pixel_grad,
        s_patch,
        own[behind : behind + BASE * BASE],
        own[0],
        own[1],
        own[2],
        s_proj[0],
        own[3],
        s_proj[1],
        s_proj[2],
        own[4],
        s_proj[3],
        own[ahead],
        own[ahead + 1],
        own[ahead + 2],
        s_up,
        s_up_bias,
        s_down,
        own[ahead + 3],
    )


def solution(mesh):
    rows = P(("img", "strip"))
    split_rows = P(("img", "strip"), None)
    split_columns = P(None, ("img", "strip"))
    held = P("img", "strip", None, None)
    return jax.shard_map(
        body,
        mesh=mesh,
        in_specs=(
            held,
            held,
            P(),
            P(),
            P(),
            P(),
            split_rows,
            split_columns,
            rows,
            rows,
            rows,
            split_rows,
            rows,
            split_rows,
            split_rows,
            rows,
            split_rows,
            rows,
            rows,
            rows,
            split_rows,
            rows,
            split_rows,
            rows,
        ),
        out_specs=(
            held,
            held,
            split_rows,
            split_columns,
            rows,
            rows,
            rows,
            split_rows,
            rows,
            split_rows,
            split_rows,
            rows,
            split_rows,
            rows,
            rows,
            rows,
            split_rows,
            rows,
            split_rows,
            rows,
        ),
        check_vma=False,
    )
```

time: 723 us -> 525 us (0.73)
  matrix products: 159 us -> 0 us
  Pallas kernels: 28.1 us -> 167 us
  local copies, waits for them, and re-layouts: 125 us -> 65.9 us
  starting transfers between devices: 126 us -> 72.8 us
  between operations: 35.6 us -> 2.07 us
  other arithmetic: 91.4 us -> 69.9 us
  waiting for transfers between devices: 150 us -> 139 us
    pallas_call x0 -> x17, Pallas kernels: none -> 167 us  [the longest x3 26 us: weight_grad(): pl.pallas_call(weight_grad_kernel, grid_spec=pltpu.PrefetchScalarGridSpec...]
    dot_general x33 -> x0, matrix products: 148 us -> none  [the longest x7 33.1 us: right_trans(): lax.dot_general(left, right, (((1,), (1,)), ((), ())), preferred_element_...]
    ppermute x30 -> x2, starting transfers between devices: 54.9 us -> 0.33 us  [along_z(): lax.ppermute(values, 'strip', [(z, z ^ r) for z in range(self.strips)])]
    all_to_all x0 -> x9, waiting for transfers between devices: none -> 54.2 us  [exchange(): return lax.all_to_all(values, 'strip', 0, 0, tiled=True)]
    ppermute x16 -> x0, waiting for transfers between devices: 46.9 us -> none  [the longest x6 26 us: to_image(): blocks.append(lax.ppermute(send, AXES, place.route(r, False)))]
    all_to_all x0 -> x9, starting transfers between devices: none -> 40.8 us  [exchange(): return lax.all_to_all(values, 'strip', 0, 0, tiled=True)]
    all_gather x4 -> x0, waiting for transfers between devices: 39 us -> none  [the longest x1 37.9 us: body(): w_down = lax.all_gather(down_weight, AXES, axis=0, tiled=True)]
    convert_element_type x9 -> x1, other arithmetic: 37.7 us -> 0.5 us  [body(): table = flat.reshape(devices, 16, TABLE // 16, lane)[..., :shard].transpo...]
  transfers between devices with their start and end apart: 79 -> 60, of which waited for: 30 -> 29; matrix products, arithmetic and copies ran while one was open for 34% -> 21% of each run, Pallas kernels for 4% -> 27%
where the time goes in v2:
time: 525 us; the launch traced here: 516 us
  Pallas kernels  167 us (32%)
  waiting for transfers between devices  139 us (26%)
  starting transfers between devices  72.8 us (14%)
  other arithmetic  69.9 us (13%)
  local copies, waits for them, and re-layouts  65.9 us (13%)
    all_to_all x9, waiting for transfers between devices, exchange(): return lax.all_to_all(values, 'strip', 0, 0, tiled=True)  54.2 us
    ppermute x26, waiting for transfers between devices, across_img(): lax.ppermute(values, 'img', [(i, i ^ bit) for i in range(self.images)])  44 us
    all_to_all x9, starting transfers between devices, exchange(): return lax.all_to_all(values, 'strip', 0, 0, tiled=True)  40.8 us
    select_n x16, other arithmetic, join(): jnp.where(where, jnp.expand_dims(mine, axis), jnp.expand_dims(other, axis))  31.5 us
    ppermute x26, starting transfers between devices, across_img(): lax.ppermute(values, 'img', [(i, i ^ bit) for i in range(self.images)])  27.4 us
    ppermute x2, waiting for transfers between devices, along_z(): lax.ppermute(values, 'strip', [(z, z ^ r) for z in range(self.strips)])  26.2 us
    pallas_call x3, Pallas kernels, weight_grad(): pl.pallas_call(weight_grad_kernel, grid_spec=pltpu.PrefetchScalarGridSpec...  26 us
    pallas_call x1, Pallas kernels, attend_back(): pl.pallas_call(functools.partial(attend_back_kernel, size=size, chunk=row...  19.1 us
  transfers between devices with their start and end apart: 60, of which 29 were waited for; matrix products, arithmetic and copies ran while one was open for 21% of the time, Pallas kernels for 27%

profile of v2, /device:TPU:0, one launch (start us, length us, event | category | flops | bytes accessed | tf_op | source)
XLA Modules:
  0.0 516.1 jit_solution(14083529032088102760)
XLA Ops:
  2.7 6.3 %all-to-all-start = ((bf16[4,96,768]{2,1,0:T(8,128)(2,1)}), bf16[4,96,768]{2,1,0:T(8,128)(2,1)S(1)}, u32[]{:S(2)}, u32[]{:S(2)}) async-start(bf16[4,96,768]{2,1,0:T(8,128)(2,1)} %broadcast_in_dim.650), calls=%async_computation | async-start | bytes 1179648 | tf_op jit(solution)/shard_map/all_to_all | solution.py:779
  12.0 9.8 %mix.1.base_ref = bf16[2,384,3072]{2,1,0:T(8,128)(2,1)} custom-call(s32[3]{0:T(128)} %pad_add_fusion.1.sizes_ref, f32[4,32,32]{2,1,0:T(8,128)} %table_ref.3, bf16[2,384,3072]{2,1,0:T(8,128)(2,1)} %bitcast.271), custom_call_target="tpu_custom_call" | custom-call | flops 4294967296 | bytes 1024 | tf_op jit(solution)/shard_map/mix/pallas_call | solution.py:98
  41.0 6.0 %collective-permute-done.3 = bf16[2,4,96,384]{3,2,1,0:T(8,128)(2,1)S(1)} collective-permute-done((bf16[2,4,96,384]{3,2,1,0:T(8,128)(2,1)S(1)}, bf16[2,4,96,384]{3,2,1,0:T(8,128)(2,1)S(1)}, u32[]{:S(2)}, u32[]{:S(2)}) %collective-permute-start.3) | collective-permute-done | bytes 589856 | tf_op jit(solution)/shard_map/ppermute | solution.py:759
  51.0 6.0 %all-to-all-done.1 = bf16[4,112,768]{2,1,0:T(8,128)(2,1)S(1)} async-done(((bf16[4,112,768]{2,1,0:T(8,128)(2,1)}), bf16[4,112,768]{2,1,0:T(8,128)(2,1)S(1)}, u32[]{:S(2)}, u32[]{:S(2)}) %all-to-all-start.1) | async-done | bytes 688160 | tf_op jit(solution)/shard_map/all_to_all | solution.py:779
  63.9 7.1 %collective-permute-done.6 = bf16[4,112,384]{2,1,0:T(8,128)(2,1)S(1)} collective-permute-done((bf16[4,112,384]{2,1,0:T(8,128)(2,1)S(1)}, bf16[4,112,384]{2,1,0:T(8,128)(2,1)S(1)}, u32[]{:S(2)}, u32[]{:S(2)}) %collective-permute-start.6) | collective-permute-done | bytes 344096 | tf_op jit(solution)/shard_map/ppermute | solution.py:759
  88.3 9.1 %embed_patches.1 = bf16[2,384,768]{2,1,0:T(8,128)(2,1)} custom-call(bf16[2,384,3072]{2,1,0:T(8,128)(2,1)} %mix.1.base_ref, bf16[3072,384]{1,0:T(8,128)(2,1)} %get-tuple-element.410.left_ref, bf16[3072,384]{1,0:T(8,128)(2,1)} %get-tuple-element.409.right_ref), custom_call_target="tpu_custom_call" | custom-call | flops 4294967296 | bytes 1024 | tf_op jit(solution)/shard_map/embed_patches/pallas_call | solution.py:375
  108.6 7.5 %all-to-all-done.3 = bf16[4,192,768]{2,1,0:T(8,128)(2,1)} async-done(((bf16[4,192,768]{2,1,0:T(8,128)(2,1)}), bf16[4,192,768]{2,1,0:T(8,128)(2,1)}, u32[]{:S(2)}, u32[]{:S(2)}) %all-to-all-start.3) | async-done | bytes 1179680 | tf_op jit(solution)/shard_map/all_to_all | solution.py:779
  156.9 5.2 %all-to-all-start.4 = ((bf16[4,6,32,768]{3,2,1,0:T(8,128)(2,1)}), bf16[4,6,32,768]{3,2,1,0:T(8,128)(2,1)}, u32[]{:S(2)}, u32[]{:S(2)}) async-start(bf16[4,6,32,768]{3,2,1,0:T(8,128)(2,1)} %maximum_select_fusion.1), calls=%async_computation.4 | async-start | bytes 2359296 | tf_op jit(solution)/shard_map/all_to_all | solution.py:779
  166.8 9.2 %enter.1 = (f32[512,768]{1,0:T(8,128)}, bf16[512,768]{1,0:T(8,128)(2,1)}, bf16[512,768]{1,0:T(8,128)(2,1)}, bf16[512,768]{1,0:T(8,128)(2,1)}, bf16[512,768]{1,0:T(8,128)(2,1)}) custom-call(s32[9]{0:T(128)} %pad_add_fusion.at_ref, bf16[512,768]{1,0:T(8,128)(2,1)} %bitcast.278, f32[2,512,64]{2,1,0:T(8,128)} %constant.314.clone.spread_ref, ...), custom_call_target="tpu_custom_call" | custom-call | flops 4294967296 | bytes 1024 | tf_op jit(solution)/shard_map/enter/pallas_call | solution.py:430
  195.4 14.4 %attend.1 = (bf16[512,768]{1,0:T(8,128)(2,1)}, f32[512,768]{1,0:T(8,128)}) custom-call(bf16[512,768]{1,0:T(8,128)(2,1)} %get-tuple-element.140.q_ref, bf16[512,768]{1,0:T(8,128)(2,1)} %get-tuple-element.154.ko_ref, bf16[512,768]{1,0:T(8,128)(2,1)} %copy-done.53, bf16[512,768]{1,0:T(8,128)(2,1)} %get-tuple-element.156.vo_ref, bf16[512,768]{1,0:T(8,128)(2,1)} %copy-done.54), custom_call_target="tpu_custom_call" | custom-call | flops 4294967296 | bytes 1024 | tf_op jit(solution)/shard_map/attend/pallas_call | solution.py:184
  219.2 14.8 %mlp.1 = (f32[512,768]{1,0:T(8,128)}, bf16[512,768]{1,0:T(8,128)(2,1)}, bf16[512,3072]{1,0:T(8,128)(2,1)}, f32[512,3072]{1,0:T(8,128)}, bf16[512,768]{1,0:T(8,128)(2,1)}) custom-call(bf16[512,768]{1,0:T(8,128)(2,1)} %get-tuple-element.157.attended_ref.o_ref.att_ref, f32[512,768]{1,0:T(8,128)} %get-tuple-element.158.embed_ref, f32[96,768]{1,0:T(8,128)} %copy-done.19, ...), custom_call_target="tpu_custom_call" | custom-call | flops 4294967296 | bytes 1024 | tf_op jit(solution)/shard_map/mlp/pallas_call | solution.py:493
  237.7 8.2 %weight_grad.3 = (bf16[4,1,384,768]{3,2,1,0:T(8,128)(2,1)}, f32[4,1,384,768]{3,2,1,0:T(8,128)}) custom-call(s32[9]{0:T(128)} %pad_add_fusion.at_ref, bf16[512,3072]{1,0:T(8,128)(2,1)} %get-tuple-element.164.left_ref, bf16[512,768]{1,0:T(8,128)(2,1)} %bitcast.257), custom_call_target="tpu_custom_call" | custom-call | flops 4294967296 | bytes 1024 | tf_op jit(solution)/shard_map/weight_grad/pallas_call | solution.py:686
  258.6 15.0 %mlp_back.1 = (bf16[512,3072]{1,0:T(8,128)(2,1)}, f32[512,768]{1,0:T(8,128)}, bf16[512,768]{1,0:T(8,128)(2,1)}, bf16[512,768]{1,0:T(8,128)(2,1)}, f32[16,768]{1,0:T(8,128)}) custom-call(bf16[512,768]{1,0:T(8,128)(2,1)} %bitcast.258, f32[512,3072]{1,0:T(8,128)} %get-tuple-element.176.slope_ref, f32[512,768]{1,0:T(8,128)} %get-tuple-element.177.resid_ref, ...), custom_call_target="tpu_custom_call" | custom-call | flops 4294967296 | bytes 1024 | tf_op jit(solution)/shard_map/mlp_back/pallas_call | solution.py:564
  273.6 8.0 %weight_grad.4 = (bf16[4,4,96,768]{3,2,1,0:T(8,128)(2,1)}, f32[4,4,96,768]{3,2,1,0:T(8,128)}) custom-call(s32[9]{0:T(128)} %pad_add_fusion.at_ref, bf16[512,768]{1,0:T(8,128)(2,1)} %get-tuple-element.174.left_ref, bf16[512,3072]{1,0:T(8,128)(2,1)} %get-tuple-element.178.right_ref), custom_call_target="tpu_custom_call" | custom-call | flops 1024 | bytes 1024 | tf_op jit(solution)/shard_map/weight_grad/pallas_call | solution.py:686
  302.9 19.1 %attend_back.1 = (bf16[512,768]{1,0:T(8,128)(2,1)}, f32[512,768]{1,0:T(8,128)}, bf16[512,768]{1,0:T(8,128)(2,1)}, f32[512,768]{1,0:T(8,128)}, bf16[512,768]{1,0:T(8,128)(2,1)}) custom-call(bf16[512,768]{1,0:T(8,128)(2,1)} %get-tuple-element.140.q_ref, bf16[512,768]{1,0:T(8,128)(2,1)} %get-tuple-element.154.ko_ref, bf16[512,768]{1,0:T(8,128)(2,1)} %copy-done.53, ...), custom_call_target="tpu_custom_call" | custom-call | flops 4294967296 | bytes 1024 | tf_op jit(solution)/shard_map/attend_back/pallas_call | solution.py:257
  323.1 5.1 collective-permute-done.28
  333.0 10.9 %leave.1 = (bf16[512,768]{1,0:T(8,128)(2,1)}, bf16[512,768]{1,0:T(8,128)(2,1)}, bf16[512,768]{1,0:T(8,128)(2,1)}, bf16[512,768]{1,0:T(8,128)(2,1)}, f32[8,768]{1,0:T(8,128)}, /*index=5*/f32[64,768]{1,0:T(8,128)}) custom-call(s32[9]{0:T(128)} %pad_add_fusion.at_ref, bf16[512,768]{1,0:T(8,128)(2,1)} %get-tuple-element.189.gq_ref, ...), custom_call_target="tpu_custom_call" | custom-call | flops 4294967296 | bytes 1024 | tf_op jit(solution)/shard_map/leave/pallas_call | solution.py:638
  358.6 8.9 %proj_grad.1 = (bf16[4,4,96,768]{3,2,1,0:T(8,128)(2,1)}, f32[4,4,96,768]{3,2,1,0:T(8,128)}) custom-call(s32[9]{0:T(128)} %pad_add_fusion.at_ref, bf16[512,768]{1,0:T(8,128)(2,1)} %get-tuple-element.204.in_ref, bf16[512,768]{1,0:T(8,128)(2,1)} %get-tuple-element.157.attended_ref.o_ref.att_ref, bf16[512,768]{1,0:T(8,128)(2,1)} %get-tuple-element.205.gq_ref, ...), custom_call_target="tpu_custom_call" | custom-call | flops 4294967296 | bytes 1024 | tf_op jit(solution)/shard_map/proj_grad/pallas_call | solution.py:724
  369.8 14.6 %all-to-all-done.6 = bf16[4,6,32,768]{3,2,1,0:T(8,128)(2,1)S(1)} async-done(((bf16[4,6,32,768]{3,2,1,0:T(8,128)(2,1)}), bf16[4,6,32,768]{3,2,1,0:T(8,128)(2,1)S(1)}, u32[]{:S(2)}, u32[]{:S(2)}) %all-to-all-start.6) | async-done | bytes 1179680 | tf_op jit(solution)/shard_map/all_to_all | solution.py:779
  388.6 9.8 %weight_grad.5 = (bf16[4,1,384,768]{3,2,1,0:T(8,128)(2,1)}, f32[4,1,384,768]{3,2,1,0:T(8,128)}) custom-call(s32[9]{0:T(128)} %pad_add_fusion.at_ref, bf16[768,3072]{1,0:T(8,128)(2,1)} %bitcast.277, bf16[768,768]{1,0:T(8,128)(2,1)} %bitcast.251), custom_call_target="tpu_custom_call" | custom-call | flops 4294967296 | bytes 1024 | tf_op jit(solution)/shard_map/weight_grad/pallas_call | solution.py:686
  399.5 8.8 %collective-permute-done.36 = f32[88,768]{1,0:T(8,128)S(1)} collective-permute-done((f32[88,768]{1,0:T(8,128)S(1)}, f32[88,768]{1,0:T(8,128)S(1)}, u32[]{:S(2)}, u32[]{:S(2)}) %collective-permute-start.36) | collective-permute-done | bytes 270368 | tf_op jit(solution)/shard_map/ppermute | solution.py:762
  420.2 15.8 %unmix.1 = f32[2,384,3072]{2,1,0:T(8,128)} custom-call(s32[3]{0:T(128)} %pad_add_fusion.1.sizes_ref, f32[4,32,32]{2,1,0:T(8,128)} %table_ref.3, bf16[3072,384]{1,0:T(8,128)(2,1)} %get-tuple-element.410.left_ref, bf16[3072,384]{1,0:T(8,128)(2,1)} %get-tuple-element.409.right_ref, bf16[2,384,768]{2,1,0:T(8,128)(2,1)} %bitcast.252), custom_call_target="tpu_custom_call" | custom-call | flops 4294967296 | bytes 1024 | tf_op jit(solution)/shard_map/unmix/pallas_call | solution.py:138
  448.7 17.4 %collective-permute-done.41 = f32[88,768]{1,0:T(8,128)} collective-permute-done((f32[88,768]{1,0:T(8,128)}, f32[88,768]{1,0:T(8,128)}, u32[]{:S(2)}, u32[]{:S(2)}) %collective-permute-start.41) | collective-permute-done | bytes 270368 | tf_op jit(solution)/shard_map/ppermute | solution.py:762
  495.9 18.4 %all-to-all-done.7 = bf16[4,192,768]{2,1,0:T(8,128)(2,1)S(1)} async-done(((bf16[4,192,768]{2,1,0:T(8,128)(2,1)}), bf16[4,192,768]{2,1,0:T(8,128)(2,1)S(1)}, u32[]{:S(2)}, u32[]{:S(2)}) %all-to-all-start.7) | async-done | bytes 1179680 | tf_op jit(solution)/shard_map/all_to_all | solution.py:779
  (426 shorter events, 258.4 us)
Async XLA Ops:
  72.1 27.5 %collective-permute-start.7 = (bf16[2,4,112,384]{3,2,1,0:T(8,128)(2,1)S(1)}, bf16[2,4,112,384]{3,2,1,0:T(8,128)(2,1)}, u32[]{:S(2)}, u32[]{:S(2)}) collective-permute-start(bf16[2,4,112,384]{3,2,1,0:T(8,128)(2,1)S(1)} %broadcast_select_fusion.9), channel_id=1, source_target_pairs={{0,16},{4,20},{8,24},{12,28},{16,0},{20,4},{24,8},{28,12},{1,17},{... | collective-permute-start | bytes 2064392 | tf_op jit(solution)/shard_map/ppermute | solution.py:759
  74.8 24.8 %collective-permute-start.9 = (bf16[2,4,112,384]{3,2,1,0:T(8,128)(2,1)}, bf16[2,4,112,384]{3,2,1,0:T(8,128)(2,1)}, u32[]{:S(2)}, u32[]{:S(2)}) collective-permute-start(bf16[2,4,112,384]{3,2,1,0:T(8,128)(2,1)} %broadcast_select_fusion.8), channel_id=1, source_target_pairs={{0,8},{4,12},{8,0},{12,4},{16,24},{20,28},{24,16},{28,20},{1,9},{5... | collective-permute-start | bytes 2064392 | tf_op jit(solution)/shard_map/ppermute | solution.py:759
  84.1 32.0 %all-to-all-start.3 = ((bf16[4,192,768]{2,1,0:T(8,128)(2,1)}), bf16[4,192,768]{2,1,0:T(8,128)(2,1)}, u32[]{:S(2)}, u32[]{:S(2)}) async-start(bf16[4,192,768]{2,1,0:T(8,128)(2,1)} %broadcast_in_dim.732), calls=%async_computation.3 | async-start | bytes 2359296 | tf_op jit(solution)/shard_map/all_to_all | solution.py:779
  105.6 28.3 %collective-permute-start.11 = (bf16[2,2,4,112,384]{4,3,2,1,0:T(8,128)(2,1)S(1)}, bf16[2,2,4,112,384]{4,3,2,1,0:T(8,128)(2,1)}, u32[]{:S(2)}, u32[]{:S(2)}) collective-permute-start(bf16[2,2,4,112,384]{4,3,2,1,0:T(8,128)(2,1)S(1)} %broadcast_select_fusion.3), channel_id=1, source_target_pairs={{0,4},{4,0},{8,12},{12,8},{16,20},{20,16},{24,28},{28,24},{1,5},{5... | collective-permute-start | bytes 4128776 | tf_op jit(solution)/shard_map/ppermute | solution.py:756
  105.7 29.2 %collective-permute-start.12 = (bf16[2,2,4,112,384]{4,3,2,1,0:T(8,128)(2,1)S(1)}, bf16[2,2,4,112,384]{4,3,2,1,0:T(8,128)(2,1)}, u32[]{:S(2)}, u32[]{:S(2)}) collective-permute-start(bf16[2,2,4,112,384]{4,3,2,1,0:T(8,128)(2,1)S(1)} %broadcast_select_fusion.2), channel_id=1, source_target_pairs={{0,4},{4,0},{8,12},{12,8},{16,20},{20,16},{24,28},{28,24},{1,5},{5... | collective-permute-start | bytes 4128776 | tf_op jit(solution)/shard_map/ppermute | solution.py:756
  116.1 33.8 %all-to-all-start.2 = ((bf16[4,6,32,768]{3,2,1,0:T(8,128)(2,1)}), bf16[4,6,32,768]{3,2,1,0:T(8,128)(2,1)}, u32[]{:S(2)}, u32[]{:S(2)}) async-start(bf16[4,6,32,768]{3,2,1,0:T(8,128)(2,1)} %maximum_select_fusion), calls=%async_computation.2 | async-start | bytes 2359296 | tf_op jit(solution)/shard_map/all_to_all | solution.py:779
  151.3 28.4 %collective-permute-start.16 = (bf16[2,4,96,768]{3,2,1,0:T(8,128)(2,1)S(1)}, bf16[2,4,96,768]{3,2,1,0:T(8,128)(2,1)S(1)}, u32[]{:S(2)}, u32[]{:S(2)}) collective-permute-start(bf16[2,4,96,768]{3,2,1,0:T(8,128)(2,1)S(1)} %broadcast_select_fusion.5), channel_id=1, source_target_pairs={{0,8},{4,12},{8,0},{12,4},{16,24},{20,28},{24,16},{28,20},{1,9},{5... | collective-permute-start | bytes 3538952 | tf_op jit(solution)/shard_map/ppermute | solution.py:759
  153.3 28.2 %collective-permute-start.18 = (bf16[2,4,96,768]{3,2,1,0:T(8,128)(2,1)S(1)}, bf16[2,4,96,768]{3,2,1,0:T(8,128)(2,1)}, u32[]{:S(2)}, u32[]{:S(2)}) collective-permute-start(bf16[2,4,96,768]{3,2,1,0:T(8,128)(2,1)S(1)} %broadcast_select_fusion.4), channel_id=1, source_target_pairs={{0,16},{4,20},{8,24},{12,28},{16,0},{20,4},{24,8},{28,12},{1,17},{... | collective-permute-start | bytes 3538952 | tf_op jit(solution)/shard_map/ppermute | solution.py:759
  156.9 34.0 %all-to-all-start.4 = ((bf16[4,6,32,768]{3,2,1,0:T(8,128)(2,1)}), bf16[4,6,32,768]{3,2,1,0:T(8,128)(2,1)}, u32[]{:S(2)}, u32[]{:S(2)}) async-start(bf16[4,6,32,768]{3,2,1,0:T(8,128)(2,1)} %maximum_select_fusion.1), calls=%async_computation.4 | async-start | bytes 2359296 | tf_op jit(solution)/shard_map/all_to_all | solution.py:779
  253.5 35.3 %all-to-all-start.5 = ((bf16[4,6,32,768]{3,2,1,0:T(8,128)(2,1)}), bf16[4,6,32,768]{3,2,1,0:T(8,128)(2,1)}, u32[]{:S(2)}, u32[]{:S(2)}) async-start(bf16[4,6,32,768]{3,2,1,0:T(8,128)(2,1)} %spread_rows.2), calls=%async_computation.5 | async-start | bytes 2359296 | tf_op jit(solution)/shard_map/all_to_all | solution.py:779
  257.9 28.3 %collective-permute-start.26 = (bf16[2,1,384,768]{3,2,0,1:T(8,128)(2,1)S(1)}, bf16[2,1,384,768]{3,2,0,1:T(8,128)(2,1)S(1)}, u32[]{:S(2)}, u32[]{:S(2)}) collective-permute-start(bf16[2,1,384,768]{3,2,0,1:T(8,128)(2,1)S(1)} %fusion), channel_id=1, source_target_pairs={{0,16},{4,20},{8,24},{12,28},{16,0},{20,4},{24,8},{28,12},{1,17},{... | collective-permute-start | bytes 3538952 | tf_op jit(solution)/shard_map/ppermute | solution.py:759
  299.9 28.3 %collective-permute-start.28 = (bf16[2,4,96,768]{3,2,1,0:T(8,128)(2,1)}, bf16[2,4,96,768]{3,2,1,0:T(8,128)(2,1)}, u32[]{:S(2)}, u32[]{:S(2)}) collective-permute-start(bf16[2,4,96,768]{3,2,1,0:T(8,128)(2,1)} %fusion.1), channel_id=1, source_target_pairs={{0,16},{4,20},{8,24},{12,28},{16,0},{20,4},{24,8},{28,12},{1,17},{... | collective-permute-start | bytes 3538952 | tf_op jit(solution)/shard_map/ppermute | solution.py:759
  350.7 33.7 %all-to-all-start.6 = ((bf16[4,6,32,768]{3,2,1,0:T(8,128)(2,1)}), bf16[4,6,32,768]{3,2,1,0:T(8,128)(2,1)S(1)}, u32[]{:S(2)}, u32[]{:S(2)}) async-start(bf16[4,6,32,768]{3,2,1,0:T(8,128)(2,1)} %spread_rows.3), calls=%async_computation.6 | async-start | bytes 2359296 | tf_op jit(solution)/shard_map/all_to_all | solution.py:779
  356.7 27.8 %collective-permute-start.37 = (bf16[4,96,768]{2,1,0:T(8,128)(2,1)}, bf16[4,96,768]{2,1,0:T(8,128)(2,1)}, u32[]{:S(2)}, u32[]{:S(2)}) collective-permute-start(bf16[4,96,768]{2,1,0:T(8,128)(2,1)} %fusion.3), channel_id=1, source_target_pairs={{0,8},{4,12},{8,0},{12,4},{16,24},{20,28},{24,16},{28,20},{1,9},{5... | collective-permute-start | bytes 1769480 | tf_op jit(solution)/shard_map/ppermute | solution.py:759
  384.5 24.6 %collective-permute-start.39 = (bf16[4,4,96,768]{3,2,1,0:T(8,128)(2,1)}, bf16[4,4,96,768]{3,2,1,0:T(8,128)(2,1)}, u32[]{:S(2)}, u32[]{:S(2)}) collective-permute-start(bf16[4,4,96,768]{3,2,1,0:T(8,128)(2,1)} %get-tuple-element.220), channel_id=1, source_target_pairs={{0,4},{4,0},{8,12},{12,8},{16,20},{20,16},{24,28},{28,24},{1,5},{5... | collective-permute-start | bytes 7077896 | tf_op jit(solution)/shard_map/ppermute | solution.py:756
  412.0 24.0 %collective-permute-start.48 = (bf16[2,2,96,768]{3,2,1,0:T(8,128)(2,1)S(1)}, bf16[2,2,96,768]{3,2,1,0:T(8,128)(2,1)}, u32[]{:S(2)}, u32[]{:S(2)}) collective-permute-start(bf16[2,2,96,768]{3,2,1,0:T(8,128)(2,1)S(1)} %fusion.7), channel_id=1, source_target_pairs={{0,8},{4,12},{8,0},{12,4},{16,24},{20,28},{24,16},{28,20},{1,9},{5... | collective-permute-start | bytes 1769480 | tf_op jit(solution)/shard_map/ppermute | solution.py:759
  412.7 26.7 %collective-permute-start.46 = (bf16[2,2,96,768]{3,2,1,0:T(8,128)(2,1)S(1)}, bf16[2,2,96,768]{3,2,1,0:T(8,128)(2,1)}, u32[]{:S(2)}, u32[]{:S(2)}) collective-permute-start(bf16[2,2,96,768]{3,2,1,0:T(8,128)(2,1)S(1)} %fusion.6), channel_id=1, source_target_pairs={{0,16},{4,20},{8,24},{12,28},{16,0},{20,4},{24,8},{28,12},{1,17},{... | collective-permute-start | bytes 1769480 | tf_op jit(solution)/shard_map/ppermute | solution.py:759
  418.7 50.3 %collective-permute-start.44 = (bf16[2,1,384,384]{3,2,0,1:T(8,128)(2,1)}, bf16[2,1,384,384]{3,2,0,1:T(8,128)(2,1)}, u32[]{:S(2)}, u32[]{:S(2)}) collective-permute-start(bf16[2,1,384,384]{3,2,0,1:T(8,128)(2,1)} %fusion.5), channel_id=1, source_target_pairs={{0,8},{4,12},{8,0},{12,4},{16,24},{20,28},{24,16},{28,20},{1,9},{5... | collective-permute-start | bytes 1769480 | tf_op jit(solution)/shard_map/ppermute | solution.py:759
  438.0 29.8 %collective-permute-start.49 = (bf16[2,96,768]{2,1,0:T(8,128)(2,1)}, bf16[2,96,768]{2,1,0:T(8,128)(2,1)}, u32[]{:S(2)}, u32[]{:S(2)}) collective-permute-start(bf16[2,96,768]{2,1,0:T(8,128)(2,1)} %fusion.14), channel_id=1, source_target_pairs={{0,16},{4,20},{8,24},{12,28},{16,0},{20,4},{24,8},{28,12},{1,17},{... | collective-permute-start | bytes 884744 | tf_op jit(solution)/shard_map/ppermute | solution.py:759
  442.4 25.4 %collective-permute-start.47 = (bf16[2,96,768]{2,1,0:T(8,128)(2,1)}, bf16[2,96,768]{2,1,0:T(8,128)(2,1)}, u32[]{:S(2)}, u32[]{:S(2)}) collective-permute-start(bf16[2,96,768]{2,1,0:T(8,128)(2,1)} %fusion.13), channel_id=1, source_target_pairs={{0,8},{4,12},{8,0},{12,4},{16,24},{20,28},{24,16},{28,20},{1,9},{5... | collective-permute-start | bytes 884744 | tf_op jit(solution)/shard_map/ppermute | solution.py:759
  443.0 23.1 %collective-permute-start.41 = (f32[88,768]{1,0:T(8,128)}, f32[88,768]{1,0:T(8,128)}, u32[]{:S(2)}, u32[]{:S(2)}) collective-permute-start(f32[88,768]{1,0:T(8,128)} %add.238), channel_id=1, source_target_pairs={{0,2},{1,3},{2,0},{3,1},{4,6},{5,7},{6,4},{7,5},{8,10},{9,11},{10,... | collective-permute-start | bytes 811016 | tf_op jit(solution)/shard_map/ppermute | solution.py:762
  443.2 27.4 %collective-permute-start.40 = (bf16[2,1,384,384]{3,2,0,1:T(8,128)(2,1)}, bf16[2,1,384,384]{3,2,0,1:T(8,128)(2,1)}, u32[]{:S(2)}, u32[]{:S(2)}) collective-permute-start(bf16[2,1,384,384]{3,2,0,1:T(8,128)(2,1)} %fusion.4), channel_id=1, source_target_pairs={{0,16},{4,20},{8,24},{12,28},{16,0},{20,4},{24,8},{28,12},{1,17},{... | collective-permute-start | bytes 1769480 | tf_op jit(solution)/shard_map/ppermute | solution.py:759
  444.7 38.1 %all-to-all-start.8 = ((bf16[4,192,768]{2,1,0:T(8,128)(2,1)}), bf16[4,192,768]{2,1,0:T(8,128)(2,1)S(1)}, u32[]{:S(2)}, u32[]{:S(2)}) async-start(bf16[4,192,768]{2,1,0:T(8,128)(2,1)} %pad_maximum_fusion), calls=%async_computation.8 | async-start | bytes 2359296 | tf_op jit(solution)/shard_map/all_to_all | solution.py:779
  482.9 31.4 %all-to-all-start.7 = ((bf16[4,192,768]{2,1,0:T(8,128)(2,1)}), bf16[4,192,768]{2,1,0:T(8,128)(2,1)S(1)}, u32[]{:S(2)}, u32[]{:S(2)}) async-start(bf16[4,192,768]{2,1,0:T(8,128)(2,1)} %pad_maximum_fusion.3), calls=%async_computation.7 | async-start | bytes 2359296 | tf_op jit(solution)/shard_map/all_to_all | solution.py:779
  (107 other events, 1071.6 us)
